TPU v7x, 32 devices: a whole 2x2x4 slice. The times are simulated.
32 devices in a mesh: dp: 8 (over y, x, core), mp: 4 (over z).
Axes of the slice: x: 2, y: 2, z: 4, core: 2. Of those that a mesh axis runs over, the one named last changes fastest.
Arguments:
- tokens: bfloat16 [8192, 1024], P('dp'), may hold values from -6 to 6
- lengths: int32 [8], P('dp'), may hold values from 1 to 1024, as said below
- w_qkv: float32 [1024, 3072], P('dp'), may hold values from -0.1875 to 0.1875
- w_out: float32 [1024, 1024], P('dp'), may hold values from -1 to 1
- ln1_gain: float32 [1024], P('dp'), may hold values from 0.5 to 1.5
- ln2_gain: float32 [1024], P('dp'), may hold values from 0.5 to 1.5
- w_in: float32 [1024, 4096], P('dp', 'mp'), may hold values from -0.1875 to 0.1875
- b_in: float32 [4096], P(('mp', 'dp')), may hold values from -3 to 3
- w_back: float32 [4096, 1024], P('mp', 'dp'), may hold values from -0.09375 to 0.09375
- b_back: float32 [1024], P('dp'), may hold values from -2 to 2
- cotangent: bfloat16 [8192, 1024], P('dp'), may hold values from -6 to 6
Outputs:
- output: bfloat16 [8192, 1024], P('dp')
- grad_tokens: float32 [8192, 1024], P('dp')
- grad_w_qkv: float32 [1024, 3072], P('dp')
- grad_w_out: float32 [1024, 1024], P('dp')
- grad_ln1_gain: float32 [1024], P('dp')
- grad_ln2_gain: float32 [1024], P('dp')
- grad_w_in: float32 [1024, 4096], P('dp', 'mp')
- grad_b_in: float32 [4096], P(('mp', 'dp'))
- grad_w_back: float32 [4096, 1024], P('mp', 'dp')
- grad_b_back: float32 [1024], P('dp')
Inputs may be any that keep to these rules, and one draw needn't show every extreme that they name: `lengths`: each image's pixels fill the start of its slot of 1024 rows; every index of dp holds at least one image of exactly 1024 pixels.
All inputs are finite; a program needn't handle non-finite values.
Results may differ from a plain program's by a relative error of at most 0.012.
Values may be sent and summed in bfloat16 or wider, within the bound.
No kernel may reach another device: no remote copies, remote signals or barrier semaphores. Data moves between devices by JAX's collectives and lax.ppermute only.
A program may use at most 192 MiB of HBM per device.

v0:
```python
import functools

import jax
import jax.numpy as jnp
from jax import lax
from jax.experimental import pallas as pl
from jax.experimental.pallas import tpu as pltpu
from jax.sharding import PartitionSpec as P

HD = 64
PAIR = 2 * HD
CHUNK = 256
EPS = 1e-05
PAIRED = 8
F32 = jnp.float32
BF16 = jnp.bfloat16
VMEM_LIMIT = 16 * 1024 * 1024
GELU_A = 0.7978845608028654
GELU_B = 0.044715


def cost(gflop, mbytes):
    return pl.CostEstimate(
        flops=int(gflop * 1e9), bytes_accessed=int(mbytes * 1e6), transcendentals=0
    )


ANY = pl.BlockSpec(memory_space=pl.ANY)
SMEM = pl.BlockSpec(memory_space=pltpu.SMEM)
VMEM = pl.BlockSpec(memory_space=pltpu.VMEM)


def nn(left, right):
    return jnp.dot(left, right, preferred_element_type=F32)


def nt(left, right):
    return lax.dot_general(left, right, (((1,), (1,)), ((), ())), preferred_element_type=F32)


def tn(left, right):
    return lax.dot_general(left, right, (((0,), (0,)), ((), ())), preferred_element_type=F32)


def normalize(values):
    centre = jnp.mean(values, -1, keepdims=True)
    centred = values - centre
    spread = jnp.mean(centred * centred, -1, keepdims=True)
    factor = lax.rsqrt(spread + EPS)
    return centred * factor, factor


def norm_back(grad, normed, factor):
    return factor * (
        grad
        - jnp.mean(grad, -1, keepdims=True)
        - normed * jnp.mean(grad * normed, -1, keepdims=True)
    )


def owner_of(base, k):
    near = 2 + 2 * (base & 1)
    chip = (0, near, 6 - near, 6)[k >> 1]
    return base ^ (chip if k & 1 == 0 else ((0, 6 - near, near, 6)[k >> 1] ^ 1))


def piece_copies(base, pieces, dst, sems, place=None, cols=None):
    copies = []
    size = dst.shape[0] // len(pieces)
    for k, piece in enumerate(pieces):
        if len(pieces) == 1:
            at = 0
        else:
            owner = owner_of(base, k)
            at = pl.multiple_of((owner if place is None else place(owner)) * size, size)
        start, width = (0, piece.shape[1]) if cols is None else cols
        copies.append(
            pltpu.make_async_copy(
                piece.at[pl.ds(0, size), pl.ds(start, width)], dst.at[pl.ds(at, size)], sems.at[k]
            )
        )
    return copies


def start_all(copies):
    for copy in copies:
        copy.start()


def wait_all(copies):
    for copy in copies:
        copy.wait()


def keep_of(length, start, rows):
    position = lax.broadcasted_iota(jnp.int32, (rows, 1), 0) + start
    return (position < length).astype(F32)


def lane_masks():
    lane = lax.broadcasted_iota(jnp.int32, (CHUNK, PAIR), 1)
    first = (lane < HD).astype(F32)
    return first.astype(BF16), (1.0 - first).astype(BF16)


def block_mask():
    row = lax.broadcasted_iota(jnp.int32, (PAIR, 2 * PAIR), 0)
    col = lax.broadcasted_iota(jnp.int32, (PAIR, 2 * PAIR), 1)
    return ((row < HD) == (col < PAIR)).astype(F32)


def split(state):
    high = state.astype(BF16)
    return high, (state - high.astype(F32)).astype(BF16)


def pair_of(arr, p):
    return arr[:, p * PAIR : (p + 1) * PAIR]


def prep_first_kernel(groups, per, vec_rows, meta, w_qkv, *refs):
    vectors, out = refs[:-1], refs[-1]
    rows, full = w_qkv.shape[0], w_qkv.shape[1] // 3
    width = full // groups
    for j in range(per):
        group = lax.rem(meta[1] + j, groups)
        for t in range(3):
            cols = pl.ds(pl.multiple_of(t * full + group * width, width), width)
            out[pl.ds(0, rows), pl.ds((3 * j + t) * width, width)] = w_qkv[:, cols].astype(BF16)
    if vec_rows:
        highs, mids, lows = [], [], []
        for vector in vectors:
            value = vector[...]
            high = value.astype(BF16).astype(F32)
            middle = (value - high).astype(BF16).astype(F32)
            highs.append(high)
            mids.append(middle)
            lows.append(value - high - middle)
        row = jnp.concatenate(highs + mids + lows, 1)
        out[pl.ds(rows, vec_rows), :] = jnp.broadcast_to(row, (vec_rows, row.shape[1])).astype(
            BF16
        )


def prep_first(meta, groups, per, vec_rows, w_qkv, vectors):
    rows, full = w_qkv.shape
    return pl.pallas_call(
        functools.partial(prep_first_kernel, groups, per, vec_rows),
        out_shape=jax.ShapeDtypeStruct((rows + vec_rows, per * full // groups), BF16),
        in_specs=[SMEM] + [VMEM] * (1 + len(vectors)),
        out_specs=VMEM,
        compiler_params=pltpu.CompilerParams(vmem_limit_bytes=VMEM_LIMIT),
        cost_estimate=cost(0.001, 3),
        name="prep_first",
    )(meta, w_qkv, *vectors)


def prep_rest_kernel(groups, per, bundles, meta, w_qkv, w_out, w_in, w_back, *outs):
    full = w_qkv.shape[1] // 3
    width = full // groups
    for b in range(bundles):
        for j in range(per):
            group = lax.rem(meta[1] + (b + 1) * per + j, groups)
            for t in range(3):
                cols = pl.ds(pl.multiple_of(t * full + group * width, width), width)
                outs[b][:, pl.ds((3 * j + t) * width, width)] = w_qkv[:, cols].astype(BF16)
    out = outs[bundles]
    hidden = w_in.shape[1]
    out[:, pl.ds(0, full)] = w_out[...].astype(BF16)
    out[:, pl.ds(full, hidden)] = w_in[...].astype(BF16)
    step = min(hidden, 256)
    for s in range(hidden // step):
        out[:, pl.ds(full + hidden + s * step, step)] = jnp.transpose(
            w_back[pl.ds(s * step, step), :]
        ).astype(BF16)


def prep_rest(meta, groups, per, w_qkv, w_out, w_in, w_back):
    rows, full = w_qkv.shape
    bundles = groups // per - 1
    shapes = [jax.ShapeDtypeStruct((rows, per * full // groups), BF16)] * bundles
    shapes.append(jax.ShapeDtypeStruct((rows, full // 3 + 2 * w_in.shape[1]), BF16))
    return pl.pallas_call(
        functools.partial(prep_rest_kernel, groups, per, bundles),
        out_shape=tuple(shapes),
        in_specs=[SMEM] + [VMEM] * 4,
        out_specs=(VMEM,) * len(shapes),
        compiler_params=pltpu.CompilerParams(vmem_limit_bytes=VMEM_LIMIT),
        cost_estimate=cost(0.001, 5),
        name="prep_rest",
    )(meta, w_qkv, w_out, w_in, w_back)


def attn_fwd_kernel(n_pieces, count_vec, start, meta, source, *refs):
    pieces = refs[:n_pieces]
    fq_out, fk_out, val_out, att_out, rden_out = refs[n_pieces : n_pieces + 5]
    rest = refs[n_pieces + 5 :]
    if count_vec:
        attn_in, vec_out, weight, states, sems, vec_scr, vec_sems = rest
    else:
        weight, states, sems = rest
        attn_in = source
    width = fq_out.shape[1]
    pairs = width // PAIR

    @pl.when(pl.program_id(0) == 0)
    def _():
        copies = piece_copies(meta[0], pieces, weight, sems, None, (start, 3 * width))
        moves = []
        if count_vec:
            size = vec_out.shape[1] // n_pieces
            moves = [
                pltpu.make_async_copy(
                    piece.at[pl.ds(size, vec_scr.shape[1])], vec_scr.at[k], vec_sems.at[k]
                )
                for k, piece in enumerate(pieces)
            ]
        start_all(moves + copies)
        for k, move in enumerate(moves):
            move.wait()
            value = vec_scr[k].astype(F32)[0:1]
            at = pl.ds(pl.multiple_of(owner_of(meta[0], k) * size, size), size)
            for a in range(count_vec):
                parts = [
                    value[:, (t * count_vec + a) * size : (t * count_vec + a + 1) * size]
                    for t in range(3)
                ]
                vec_out[a : a + 1, at] = parts[0] + parts[1] + parts[2]
        states[...] = jnp.zeros_like(states)
        wait_all(copies)

    if count_vec:
        attn_in[...] = (source[...] * vec_out[0:1, :]).astype(BF16)
    mask_a, mask_b = lane_masks()
    blocks = block_mask()
    first = lax.broadcasted_iota(jnp.int32, (CHUNK, PAIR), 1) < HD
    causal = lax.broadcasted_iota(jnp.int32, (CHUNK, CHUNK), 0) >= lax.broadcasted_iota(
        jnp.int32, (CHUNK, CHUNK), 1
    )
    proj = nn(attn_in[...], weight[...])
    query, keys = proj[:, :width], proj[:, width : 2 * width]
    fq = jnp.where(query > 0, query + 1.0, jnp.exp(jnp.minimum(query, 0.0))).astype(BF16)
    fk = jnp.where(keys > 0, keys + 1.0, jnp.exp(jnp.minimum(keys, 0.0))).astype(BF16)
    val = proj[:, 2 * width :].astype(BF16)
    fq_out[...] = fq
    fk_out[...] = fk
    val_out[...] = val
    for p in range(pairs):
        q, k, v = pair_of(fq, p), pair_of(fk, p), pair_of(val, p)
        v_a = v * mask_a + mask_b
        v_b = v * mask_b + mask_a
        s_a = jnp.where(causal, nt(q * mask_a, k), 0.0).astype(BF16)
        s_b = jnp.where(causal, nt(q * mask_b, k), 0.0).astype(BF16)
        high, low = split(states[p])
        past = nn(q, high) + nn(q, low)
        r_a = nn(s_a, v_a) + past[:, :PAIR]
        r_b = nn(s_b, v_b) + past[:, PAIR:]
        numer = jnp.where(first, r_a, r_b)
        denom = pltpu.roll(jnp.where(first, r_b, r_a), HD, axis=1)
        inverse = 1.0 / denom
        cols = pl.ds(p * PAIR, PAIR)
        att_out[:, cols] = (numer * inverse).astype(BF16)
        rden_out[:, cols] = inverse
        states[p] = states[p] + tn(k, jnp.concatenate([v_a, v_b], 1)) * blocks


def attn_fwd(meta, source, pieces, groups, position, count_vec):
    rows, full = source.shape
    width = full // groups
    n = len(pieces)
    low = jax.ShapeDtypeStruct((rows, width), BF16)
    shapes = [low, low, low, low, jax.ShapeDtypeStruct((rows, width), F32)]
    specs = [pl.BlockSpec((CHUNK, width), lambda i: (i, 0))] * 5
    wide = pl.BlockSpec((CHUNK, full), lambda i: (i, 0))
    scratch = [
        pltpu.VMEM((full, 3 * width), BF16),
        pltpu.VMEM((width // PAIR, PAIR, 2 * PAIR), F32),
        pltpu.SemaphoreType.DMA((n,)),
    ]
    if count_vec:
        shapes += [
            jax.ShapeDtypeStruct((rows, full), BF16),
            jax.ShapeDtypeStruct((count_vec, full), F32),
        ]
        specs += [wide, pl.BlockSpec((count_vec, full), lambda i: (0, 0))]
        vec_rows = pieces[0].shape[0] - full // n
        scratch += [
            pltpu.VMEM((n, vec_rows, pieces[0].shape[1]), BF16),
            pltpu.SemaphoreType.DMA((n,)),
        ]
    return pl.pallas_call(
        functools.partial(attn_fwd_kernel, n, count_vec, position * 3 * width),
        grid=(rows // CHUNK,),
        out_shape=tuple(shapes),
        in_specs=[SMEM, wide] + [ANY] * n,
        out_specs=tuple(specs),
        scratch_shapes=scratch,
        compiler_params=pltpu.CompilerParams(vmem_limit_bytes=VMEM_LIMIT),
        cost_estimate=cost(8, 6),
        name="attn_fwd",
    )(meta, source, *pieces)


def rest_copies(meta, which, pieces, dst, sems, groups):
    n = len(pieces)
    full = dst.shape[0]
    if which:
        hidden = dst.shape[1]
        cols = (full + (which - 1) * hidden, hidden)
        return piece_copies(meta[0], pieces, dst, sems.at[which], None, cols)
    width = full // groups
    if n == 1:
        found = []
        for j in range(groups):
            at = pl.multiple_of(lax.rem(meta[1] + j, groups) * width, width)
            found.append(
                pltpu.make_async_copy(
                    pieces[0].at[pl.ds(at, width), pl.ds(0, full)],
                    dst.at[pl.ds(j * width, width)],
                    sems.at[0, j],
                )
            )
        return found
    span = n // groups

    def turned(owner):
        group = lax.rem(owner // span - meta[1] + groups, groups)
        return group * span + lax.rem(owner, span)

    return piece_copies(meta[0], pieces, dst, sems.at[0], turned, (0, full))


def mlp_kernel(n_pieces, n_atts, groups, part, meta, *refs):
    atts = refs[:n_atts]
    tok, cot, vec, bias = refs[n_atts : n_atts + 4]
    pieces = refs[n_atts + 4 : n_atts + 4 + n_pieces]
    refs = refs[n_atts + 4 + n_pieces :]
    send_out, keep_out, hidden_out, gpre_out, min_out, resid_out = refs[:6]
    w_o, w_i, w_b, sems = refs[6:]
    i = pl.program_id(0)

    def loads(which):
        return rest_copies(meta, which, pieces, (w_o, w_i, w_b)[which], sems, groups)

    @pl.when(i == 0)
    def _():
        for which in range(3):
            start_all(loads(which))
        wait_all(loads(0))

    gain = vec[1:2, :]
    start = (2 * part + (i ^ (1 - meta[3]))) * CHUNK
    keep = keep_of(meta[2], start, CHUNK)
    g_low = (cot[...].astype(F32) * keep).astype(BF16)
    mixed = nn(jnp.concatenate([att[...] for att in atts], 1), w_o[...])
    resid = tok[...].astype(F32) + mixed
    resid_out[...] = resid
    normed, _ = normalize(resid)
    mlp_in = (normed * gain).astype(BF16)
    min_out[...] = mlp_in

    @pl.when(i == 0)
    def _():
        wait_all(loads(1))
        wait_all(loads(2))

    pre = nn(mlp_in, w_i[...]) + bias[...]
    square = pre * pre
    t = jnp.tanh(GELU_A * pre * (1.0 + GELU_B * square))
    half = 0.5 * (1.0 + t)
    hidden_out[...] = (pre * half).astype(BF16)
    slope = half + (0.5 * GELU_A) * pre * (1.0 - t * t) * (1.0 + (3.0 * GELU_B) * square)
    gpre = (nn(g_low, w_b[...]) * slope).astype(BF16)
    gpre_out[...] = gpre
    grad = nt(gpre, w_i[...]).astype(BF16)

    @pl.when(i == 0)
    def _():
        send_out[...] = grad

    @pl.when(i == 1)
    def _():
        keep_out[...] = grad


def mlp(meta, part, atts, groups, tokens, cotangent, vec, bias, pieces):
    n, n_atts = len(pieces), len(atts)
    rows = 2 * CHUNK
    width, hidden = tokens.shape[1], bias.shape[1]

    def rowed(cols, base):
        return pl.BlockSpec((CHUNK, cols), lambda i, m: (base + (i ^ (1 - m[3])), 0))

    def whole(shape):
        return pl.BlockSpec(shape, lambda i, m: (0, 0))

    shapes = [(CHUNK, width), (CHUNK, width), (rows, hidden), (rows, hidden), (rows, width)]
    return pl.pallas_call(
        functools.partial(mlp_kernel, n, n_atts, groups, part),
        out_shape=tuple(jax.ShapeDtypeStruct(shape, BF16) for shape in shapes)
        + (jax.ShapeDtypeStruct((rows, width), F32),),
        grid_spec=pltpu.PrefetchScalarGridSpec(
            num_scalar_prefetch=1,
            grid=(2,),
            in_specs=[rowed(a.shape[1], 2 * part) for a in atts]
            + [rowed(width, 2 * part)] * 2
            + [whole(vec.shape), whole(bias.shape)]
            + [ANY] * n,
            out_specs=(
                whole((CHUNK, width)),
                whole((CHUNK, width)),
                rowed(hidden, 0),
                rowed(hidden, 0),
                rowed(width, 0),
                rowed(width, 0),
            ),
            scratch_shapes=[
                pltpu.VMEM((width, width), BF16),
                pltpu.VMEM((width, hidden), BF16),
                pltpu.VMEM((width, hidden), BF16),
                pltpu.SemaphoreType.DMA((3, max(n, groups))),
            ],
        ),
        compiler_params=pltpu.CompilerParams(vmem_limit_bytes=VMEM_LIMIT),
        cost_estimate=cost(8, 16),
        name="mlp_fwd_bwd",
    )(meta, *atts, tokens, cotangent, vec, bias, *pieces)


def mlp_out_kernel(n_pieces, parts, meta, *refs):
    hiddens = refs[:parts]
    pieces = refs[parts : parts + n_pieces]
    send, keep, w_b, sems = refs[parts + n_pieces :]
    copies = rest_copies(meta, 2, pieces, w_b, sems, 1)
    start_all(copies)
    wait_all(copies)
    for c, out in enumerate((send, keep)):
        at = pl.multiple_of((c ^ (1 - meta[3])) * CHUNK, CHUNK)
        for r in range(parts):
            out[pl.ds(r * CHUNK, CHUNK), :] = nt(hiddens[r][pl.ds(at, CHUNK), :], w_b[...]).astype(
                BF16
            )


def mlp_out(meta, hiddens, pieces, width):
    n, parts = len(pieces), len(hiddens)
    hidden = hiddens[0].shape[1]
    return pl.pallas_call(
        functools.partial(mlp_out_kernel, n, parts),
        out_shape=(jax.ShapeDtypeStruct((parts * CHUNK, width), BF16),) * 2,
        in_specs=[SMEM] + [VMEM] * parts + [ANY] * n,
        out_specs=(VMEM,) * 2,
        scratch_shapes=[
            pltpu.VMEM((width, hidden), BF16),
            pltpu.SemaphoreType.DMA((3, n)),
        ],
        compiler_params=pltpu.CompilerParams(vmem_limit_bytes=VMEM_LIMIT),
        cost_estimate=cost(4, 8),
        name="mlp_out",
    )(meta, *hiddens, *pieces)


def offset_of(n_blocks, base, k, size):
    return pl.multiple_of((base ^ k) * size, size) if n_blocks == PAIRED else k * size


def spread(n_blocks, base, scratch, own, sib, start):
    size = own.shape[1]
    cols = pl.ds(start, scratch.shape[1])
    for k in range(n_blocks):
        at = offset_of(n_blocks, base, k, size)
        (own, sib)[k & 1][k >> 1, :, cols] = scratch[pl.ds(at, size), :]


def mlp_grads_kernel(n_blocks, parts, meta, *refs):
    hiddens, gpres, mins = (refs[a * parts : (a + 1) * parts] for a in range(3))
    cot = refs[3 * parts]
    own, sib, bin_out, bback_out, scratch, g_low = refs[3 * parts + 1 :]
    rows = hiddens[0].shape[0]
    total_in = total_back = None
    for r in range(parts):
        keep = keep_of(meta[2], r * rows, rows)
        g = cot[pl.ds(r * rows, rows), :].astype(F32) * keep
        g_low[pl.ds(r * rows, rows), :] = g.astype(BF16)
        back = jnp.sum(g, 0, keepdims=True)
        inner = jnp.sum(gpres[r][...].astype(F32), 0, keepdims=True)
        total_in = inner if total_in is None else total_in + inner
        total_back = back if total_back is None else total_back + back
    bin_out[...] = total_in
    bback_out[...] = total_back
    step = 256
    hidden = hiddens[0].shape[1]
    for s in range(scratch.shape[0] // step):
        cols = pl.ds(s * step, step)
        up = down = None
        for r in range(parts):
            part = tn(mins[r][:, cols], gpres[r][...])
            up = part if up is None else up + part
            part = tn(g_low[pl.ds(r * rows, rows), cols], hiddens[r][...])
            down = part if down is None else down + part
        scratch[cols, pl.ds(0, hidden)] = up.astype(BF16)
        scratch[cols, pl.ds(hidden, hidden)] = down.astype(BF16)
    spread(n_blocks, meta[0], scratch, own, sib, 0)


def mlp_grads(meta, n_blocks, hiddens, gpres, mins, cotangent):
    parts = len(hiddens)
    hidden, width = hiddens[0].shape[1], mins[0].shape[1]
    blocks = jax.ShapeDtypeStruct((n_blocks // 2, width // n_blocks, 2 * hidden), BF16)
    return pl.pallas_call(
        functools.partial(mlp_grads_kernel, n_blocks, parts),
        out_shape=(
            blocks,
            blocks,
            jax.ShapeDtypeStruct((1, hidden), F32),
            jax.ShapeDtypeStruct((1, width), F32),
        ),
        in_specs=[SMEM] + [VMEM] * (3 * parts + 1),
        out_specs=(VMEM,) * 4,
        scratch_shapes=[
            pltpu.VMEM((width, 2 * hidden), BF16),
            pltpu.VMEM(cotangent.shape, BF16),
        ],
        compiler_params=pltpu.CompilerParams(vmem_limit_bytes=VMEM_LIMIT),
        cost_estimate=cost(8, 16),
        name="mlp_grads",
    )(meta, *hiddens, *gpres, *mins, cotangent)


def norm_bwd_kernel(parts, meta, *refs):
    totals = refs[: 2 * parts]
    resids = refs[2 * parts : 3 * parts]
    cot, vec, gres_out, gmix_out, gain_out = refs[3 * parts :]
    i = pl.program_id(0)
    chunk = 2 * (i // 2) + (lax.rem(i, 2) ^ meta[3])
    keep = keep_of(meta[2], chunk * CHUNK, CHUNK)

    @pl.when(i == 0)
    def _():
        gain_out[...] = jnp.zeros_like(gain_out)

    for r in range(parts):
        for h in range(2):

            @pl.when(i == 2 * r + h)
            def _():
                grad = totals[2 * r + h][...].astype(F32)
                normed, factor = normalize(resids[r][...])
                gain_out[...] += jnp.sum(grad * normed, 0, keepdims=True)
                gres = cot[...].astype(F32) * keep + norm_back(
                    grad * vec[1:2, :], normed, factor
                )
                gres_out[...] = gres
                gmix_out[...] = gres.astype(BF16)


def norm_bwd(meta, totals, resids, cotangent, vec):
    parts = len(resids)
    rows, full = cotangent.shape

    def whole(shape):
        return pl.BlockSpec(shape, lambda i, m: (0, 0))

    def inner(r):
        def index(i, m):
            bit = lax.rem(jnp.clip(i - 2 * r, 0, 1), 2)
            return (bit ^ m[3], 0)

        return pl.BlockSpec((CHUNK, full), index)

    rowed = pl.BlockSpec((CHUNK, full), lambda i, m: (2 * (i // 2) + (lax.rem(i, 2) ^ m[3]), 0))
    return pl.pallas_call(
        functools.partial(norm_bwd_kernel, parts),
        out_shape=(
            jax.ShapeDtypeStruct((rows, full), F32),
            jax.ShapeDtypeStruct((rows, full), BF16),
            jax.ShapeDtypeStruct((1, full), F32),
        ),
        grid_spec=pltpu.PrefetchScalarGridSpec(
            num_scalar_prefetch=1,
            grid=(2 * parts,),
            in_specs=[whole(t.shape) for t in totals]
            + [inner(r) for r in range(parts)]
            + [rowed, whole(vec.shape)],
            out_specs=(rowed, rowed, whole((1, full))),
        ),
        compiler_params=pltpu.CompilerParams(vmem_limit_bytes=VMEM_LIMIT),
        cost_estimate=cost(1, 16),
        name="norm_bwd",
    )(meta, *totals, *resids, cotangent, vec)


def group_rows(meta, group, width, pieces, dst, sems, start):
    full = dst.shape[1]
    if len(pieces) == 1:
        at = pl.multiple_of(group * width, width)
        copy = pltpu.make_async_copy(
            pieces[0].at[pl.ds(at, width), pl.ds(0, full)], dst, sems.at[0]
        )
        return copy.start() if start else copy.wait()
    size = pieces[0].shape[0]
    for part in range(width // size):
        wanted = group * (width // size) + part
        target = dst.at[pl.ds(part * size, size)]
        if not start:
            pltpu.make_async_copy(
                pieces[0].at[:, pl.ds(0, full)], target, sems.at[part]
            ).wait()
            continue
        for k, piece in enumerate(pieces):

            @pl.when(wanted == owner_of(meta[0], k))
            def _():
                pltpu.make_async_copy(
                    piece.at[:, pl.ds(0, full)], target, sems.at[part]
                ).start()


def attn_bwd_kernel(shape, meta, *refs):
    n, groups, position, start, n_atts, n_vectors, n_blocks = shape
    is_first, is_last = position == 0, position == groups - 1
    refs = list(refs)

    def take(count):
        found = refs[:count]
        del refs[:count]
        return found

    gmix, fq, fk, val, att, rden = take(6)
    (acc_in,) = take(1) if not is_first else (None,)
    attn_in, *atts = take(1 + n_atts) if is_first else (None,)
    tok, gres, vec, *vectors = take(3 + n_vectors) if is_last else (None, None, None)
    pieces_o, pieces_w = take(n), take(n)
    (acc_out,) = take(1)
    own, sib = take(2) if is_first or is_last else (None, None)
    w_o, w_q, state_scr, later, sems_o, sems_w = take(6)
    width = fq.shape[1]
    pairs = width // PAIR
    full = gmix.shape[1]
    i = pl.program_id(0)
    count = fk.shape[0] // CHUNK
    c = count - 1 - i
    place = meta[1]
    group = lax.rem(place + position, groups)
    mask_a, mask_b = lane_masks()
    blocks = block_mask()

    def weight_copies():
        return piece_copies(meta[0], pieces_w, w_q, sems_w, None, (start, 3 * width))

    def side_copies():
        found = [pltpu.make_async_copy(attn_in, ain_scr, side_sems.at[0])]
        for a in range(n_atts):
            found.append(
                pltpu.make_async_copy(
                    atts[a], att_scr.at[:, pl.ds(a * width, width)], side_sems.at[a + 1]
                )
            )
        return found

    if is_first:
        gproj_scr, gcol_scr, ain_scr, att_scr, product, side_sems = take(6)
    if is_last:
        (gain_scr,) = take(1)

    @pl.when(i == 0)
    def _():
        group_rows(meta, group, width, pieces_o, w_o, sems_o, True)
        start_all(weight_copies())
        if is_first:
            start_all(side_copies())
        if is_last:
            gain_scr[...] = jnp.zeros_like(gain_scr)
        later[...] = jnp.zeros_like(later)
        for p in range(pairs):
            state = jnp.zeros((PAIR, 2 * PAIR), F32)
            for s in range(count):
                high, low = split(state)
                state_scr[s, p, 0] = high
                state_scr[s, p, 1] = low
                if s + 1 < count:
                    rows, cols = pl.ds(s * CHUNK, CHUNK), pl.ds(p * PAIR, PAIR)
                    v = val[rows, cols]
                    aug = jnp.concatenate([v * mask_a + mask_b, v * mask_b + mask_a], 1)
                    state = state + tn(fk[rows, cols], aug) * blocks
        group_rows(meta, group, width, pieces_o, w_o, sems_o, False)
        wait_all(weight_copies())

    first = lax.broadcasted_iota(jnp.int32, (CHUNK, PAIR), 1) < HD
    row = lax.broadcasted_iota(jnp.int32, (CHUNK, CHUNK), 0)
    col = lax.broadcasted_iota(jnp.int32, (CHUNK, CHUNK), 1)
    causal, causal_t = row >= col, row <= col
    head_row = lax.broadcasted_iota(jnp.int32, (width, width), 0) // HD
    head_col = lax.broadcasted_iota(jnp.int32, (width, width), 1) // HD
    head_sum = (head_row == head_col).astype(F32).astype(BF16)
    rows = pl.ds(pl.multiple_of(c * CHUNK, CHUNK), CHUNK)
    grad_att = nt(gmix[...], w_o[...])
    inverse = rden[...]
    gnum = (grad_att * inverse).astype(BF16)
    dots = nn((grad_att * att[...].astype(F32)).astype(BF16), head_sum)
    gden = (-dots * inverse).astype(BF16).astype(F32)
    found_q, found_k, found_v = [], [], []
    for p in range(pairs):
        cols = pl.ds(p * PAIR, PAIR)
        q, k, v = fq[:, cols], fk[rows, cols], val[rows, cols]
        num = pair_of(gnum, p)
        den = (pltpu.roll(pair_of(gden, p), HD, axis=1) * (1.0 / HD)).astype(BF16)
        n_a, n_b = num * mask_a + den * mask_b, num * mask_b + den * mask_a
        q_a, q_b = q * mask_a, q * mask_b
        v_a, v_b = v * mask_a + mask_b, v * mask_b + mask_a
        n_cat = jnp.concatenate([n_a, n_b], 1)
        v_cat = jnp.concatenate([v_a, v_b], 1)
        st_a = jnp.where(causal_t, nt(k, q_a), 0.0).astype(BF16)
        st_b = jnp.where(causal_t, nt(k, q_b), 0.0).astype(BF16)
        gs_a = jnp.where(causal, nt(n_a, v_a), 0.0).astype(BF16)
        gs_b = jnp.where(causal, nt(n_b, v_b), 0.0).astype(BF16)
        gt_a = jnp.where(causal_t, nt(v_a, n_a), 0.0).astype(BF16)
        gt_b = jnp.where(causal_t, nt(v_b, n_b), 0.0).astype(BF16)
        high, low = split(later[p])
        past = nn(k, high) + nn(k, low)
        gq = nn(gs_a, k * mask_a) + nn(gs_b, k * mask_b)
        gq = gq + nt(n_cat, state_scr[c, p, 0]) + nt(n_cat, state_scr[c, p, 1])
        gk = nn(gt_a, q_a) + nn(gt_b, q_b) + nt(v_cat, high) + nt(v_cat, low)
        gv = nn(st_a, num * mask_a) + nn(st_b, num * mask_b)
        gv = gv + jnp.where(first, past[:, :PAIR], past[:, PAIR:])
        later[p] = later[p] + tn(q, n_cat) * blocks
        found_q.append((gq * jnp.minimum(q.astype(F32), 1.0)).astype(BF16))
        found_k.append((gk * jnp.minimum(k.astype(F32), 1.0)).astype(BF16))
        found_v.append(gv.astype(BF16))
    gproj = jnp.concatenate(found_q + found_k + found_v, 1)
    grad = nt(gproj, w_q[...])
    if not is_first:
        grad = grad + acc_in[...]
    if not is_last:
        acc_out[...] = grad
    else:
        normed, factor = normalize(tok[...].astype(F32))
        gain_scr[...] += jnp.sum(grad * normed, 0, keepdims=True)
        acc_out[...] = gres[...] + norm_back(grad * vec[0:1, :], normed, factor)

        @pl.when(i == count - 1)
        def _():
            for a, source in enumerate([gain_scr] + vectors):
                size = source.shape[1] // n_blocks
                for k in range(n_blocks):
                    at = offset_of(n_blocks, meta[0], k, size)
                    (own, sib)[k & 1][k >> 1, a : a + 1, pl.ds(0, size)] = source[
                        :, pl.ds(at, size)
                    ]

    if is_first:
        gproj_scr[rows, :] = gproj
        gcol_scr[rows, :] = gmix[:, pl.ds(pl.multiple_of(place * width, width), width)]

        @pl.when(i == count - 1)
        def _():
            wait_all(side_copies())
            for s in range(full // 256):
                piece = pl.ds(s * 256, 256)
                product[piece, pl.ds(0, 3 * width)] = tn(
                    ain_scr[:, s * 256 : (s + 1) * 256], gproj_scr[...]
                ).astype(BF16)
            for j in range(groups):
                at = pl.multiple_of(lax.rem(place + j, groups) * width, width)
                product[pl.ds(at, width), pl.ds(3 * width, width)] = tn(
                    att_scr[:, j * width : (j + 1) * width], gcol_scr[...]
                ).astype(BF16)
            spread(n_blocks, meta[0], product, own, sib, 0)


def attn_bwd(meta, n_blocks, position, start, gmix, heads, pieces_o, pieces_w, extra):
    n = len(pieces_o)
    rows, full = gmix.shape
    width = heads[0].shape[1]
    groups = full // width
    count = rows // CHUNK
    is_first, is_last = position == 0, position == groups - 1

    def rowed(cols):
        return pl.BlockSpec((CHUNK, cols), lambda i: (count - 1 - i, 0))

    def whole(shape):
        return pl.BlockSpec(shape, lambda i: (0,) * len(shape))

    specs = [rowed(full), rowed(width), whole((rows, width)), whole((rows, width))]
    specs += [rowed(width), rowed(width)]
    n_atts = n_vectors = 0
    if is_first:
        n_atts = len(extra) - 1
        specs += [ANY] * len(extra)
    else:
        specs += [rowed(full)]
    if is_last:
        n_vectors = len(extra) - 4
        specs += [rowed(full), rowed(full)] + [whole(v.shape) for v in extra[3:]]
    shapes, outs = [jax.ShapeDtypeStruct((rows, full), F32)], [rowed(full)]
    scratch = [
        pltpu.VMEM((width, full), BF16),
        pltpu.VMEM((full, 3 * width), BF16),
        pltpu.VMEM((count, width // PAIR, 2, PAIR, 2 * PAIR), BF16),
        pltpu.VMEM((width // PAIR, PAIR, 2 * PAIR), F32),
        pltpu.SemaphoreType.DMA((max(1, width * n // full),)),
        pltpu.SemaphoreType.DMA((n,)),
    ]
    if is_first:
        blocks = (n_blocks // 2, full // n_blocks, 4 * width)
        shapes += [jax.ShapeDtypeStruct(blocks, BF16)] * 2
        outs += [whole(blocks)] * 2
        scratch += [
            pltpu.VMEM((rows, 3 * width), BF16),
            pltpu.VMEM((rows, width), BF16),
            pltpu.VMEM((rows, full), BF16),
            pltpu.VMEM((rows, full), BF16),
            pltpu.VMEM((full, 4 * width), BF16),
            pltpu.SemaphoreType.DMA((n_atts + 1,)),
        ]
    if is_last:
        small = (n_blocks // 2, 4, full // n_blocks)
        shapes += [jax.ShapeDtypeStruct(small, F32)] * 2
        outs += [whole(small)] * 2
        scratch += [pltpu.VMEM((1, full), F32)]
    shape = (n, groups, position, start, n_atts, n_vectors, n_blocks)
    return pl.pallas_call(
        functools.partial(attn_bwd_kernel, shape),
        grid=(count,),
        out_shape=tuple(shapes),
        in_specs=[SMEM] + specs + [ANY] * (2 * n),
        out_specs=tuple(outs),
        scratch_shapes=scratch,
        compiler_params=pltpu.CompilerParams(vmem_limit_bytes=VMEM_LIMIT),
        cost_estimate=cost(10, 7),
        name="attn_bwd",
    )(meta, gmix, *heads, *extra, *pieces_o, *pieces_w)


def finish_kernel(parts, meta, *refs):
    resids = refs[:parts]
    kept, other, vec, out = refs[parts:]
    bias = vec[3:4, :]
    for r in range(parts):
        for source, h in ((kept, 0), (other, 1)):
            inner = pl.multiple_of((h ^ meta[3]) * CHUNK, CHUNK)
            at = pl.multiple_of(r * 2 * CHUNK + inner, CHUNK)
            summed = source[pl.ds(r * CHUNK, CHUNK), :].astype(F32)
            total = resids[r][pl.ds(inner, CHUNK), :] + (summed + bias)
            keep = keep_of(meta[2], at, CHUNK)
            out[pl.ds(at, CHUNK), :] = (total * keep).astype(BF16)


def finish(meta, resids, kept, other, vec):
    rows, width = 2 * CHUNK * len(resids), kept.shape[1]
    return pl.pallas_call(
        functools.partial(finish_kernel, len(resids)),
        out_shape=jax.ShapeDtypeStruct((rows, width), BF16),
        in_specs=[SMEM] + [VMEM] * (len(resids) + 3),
        out_specs=VMEM,
        compiler_params=pltpu.CompilerParams(vmem_limit_bytes=VMEM_LIMIT),
        cost_estimate=cost(0.01, 8),
        name="finish",
    )(meta, *resids, kept, other, vec)


def assemble_kernel(groups, turned, meta, *refs):
    pieces, (qkv, out) = refs[:-2], refs[-2:]
    width = out.shape[1] // groups
    for d, piece in enumerate(pieces):
        group = lax.rem(meta[1] - d + groups, groups) if turned else d
        for t in range(4):
            value = piece[:, pl.ds(t * width, width)].astype(F32)
            start = t % 3 * groups * width + group * width
            at = pl.ds(pl.multiple_of(start, width), width)
            (out if t == 3 else qkv)[:, at] = value


def assemble(meta, groups, turned, pieces):
    rows, width = pieces[0].shape[0], pieces[0].shape[1] // 4
    return pl.pallas_call(
        functools.partial(assemble_kernel, groups, turned),
        out_shape=(
            jax.ShapeDtypeStruct((rows, 3 * groups * width), F32),
            jax.ShapeDtypeStruct((rows, groups * width), F32),
        ),
        in_specs=[SMEM] + [VMEM] * len(pieces),
        out_specs=(VMEM,) * 2,
        compiler_params=pltpu.CompilerParams(vmem_limit_bytes=VMEM_LIMIT),
        cost_estimate=cost(0.01, 3),
        name="assemble",
    )(meta, *pieces)


def send(arr, move):
    return lax.ppermute(arr, "dp", [(i, move(i)) for i in range(PAIRED)])


def near(i):
    return i ^ (4 if i & 1 else 2)


def far(i):
    return i ^ (2 if i & 1 else 4)


def across(i):
    return i ^ 1


def after(arrs, *deps):
    return lax.optimization_barrier((arrs, deps))[0]


def gather_pieces(arr):
    one, two = send(arr, near), send(arr, far)
    three = send(one, far)
    pieces = []
    for piece in (arr, one, two, three):
        pieces += [piece, send(piece, across)]
    return pieces


def chip_sum(own, sib):
    return own.astype(F32) + send(sib, across).astype(F32)


def plane_sum(both, kind):
    total = both[0]
    for k in range(1, PAIRED // 2):
        moved = send(both[k].astype(kind), lambda i, k=k: i ^ (2 * k))
        total = total + moved.astype(F32)
    return total


def swapped(arr, bits):
    return lax.ppermute(arr, "mp", [(i, i ^ bits) for i in range(4)])


def add_low(left, right):
    return (left.astype(F32) + right.astype(F32)).astype(BF16)


def per_device(
    n_dp, n_mp, tokens, lengths, w_qkv, w_out, ln1_gain, ln2_gain, w_in, b_in, w_back, b_back,
    cotangent,
):
    rows, full = tokens.shape
    groups = n_mp
    per = 2
    paired = n_dp == PAIRED and n_mp == 4
    index = lax.axis_index("dp").astype(jnp.int32)
    place = lax.axis_index("mp").astype(jnp.int32)
    zero = jnp.zeros_like(index)
    meta = jnp.stack(
        [index if paired else zero, place, lengths[0], (place & 1) if paired else zero]
    )
    vectors = [v[None] for v in (ln1_gain, ln2_gain, b_in, b_back)]

    def gather(arr, axis=0):
        return lax.all_gather(arr, "dp", axis=axis, tiled=True)

    first_sent = prep_first(
        meta, groups, per, 16 if paired else 0, w_qkv, vectors if paired else ()
    )
    normed_one, _ = normalize(tokens.astype(F32))
    parts = rows // (2 * CHUNK)
    found, totals = [None] * parts, [None] * (2 * parts)

    if not paired:
        sent = [first_sent] + list(prep_rest(meta, groups, per, w_qkv, w_out, w_in, w_back))
        gathered = [[gather(arr)] for arr in sent]
        bundles, rest = gathered[:-1], gathered[-1]
        gain_one, gain_two, bias, bias_back = (gather(v, 1) for v in vectors)
        attn_in = (normed_one * gain_one).astype(BF16)
        vec = jnp.concatenate([gain_one, gain_two, gain_two, bias_back], 0)
        heads = [
            attn_fwd(meta, attn_in, bundles[j // per], groups, j % per, 0) for j in range(groups)
        ]
    else:
        bundles = [gather_pieces(first_sent)]
        raw = after((w_qkv, w_out, w_in, w_back), bundles[0][1])
        second, third = prep_rest(meta, groups, per, *raw)
        bundles.append(gather_pieces(second))
        rest = gather_pieces(after(third, bundles[0][2]))
        heads = [attn_fwd(meta, after(normed_one, bundles[1][2]), bundles[0], groups, 0, 4)]
        attn_in, vec = heads[0][5:]
        bias = vec[2:3]
        heads.append(attn_fwd(meta, attn_in, bundles[0], groups, 1, 0))
        attn_in = after(attn_in, rest[2])
        heads.append(attn_fwd(meta, attn_in, bundles[1], groups, 0, 0))
        heads.append(attn_fwd(meta, attn_in, bundles[1], groups, 1, 0))
    heads = [h[:5] for h in heads]
    atts = [h[3] for h in heads]

    for r in reversed(range(parts)):
        found[r] = mlp(meta, r, atts, groups, tokens, cotangent, vec, bias, rest)
    aways, keeps, hiddens, gpres, mins, resids = (list(x) for x in zip(*found))
    if paired:
        pairs = [None] * parts
        for r in reversed(range(parts)):
            pairs[r] = add_low(keeps[r], swapped(aways[r], 1))
        for r in reversed(range(parts)):
            totals[2 * r] = add_low(pairs[r], swapped(pairs[r], 2))
            totals[2 * r + 1] = swapped(totals[2 * r], 1)
    own, sib, g_bin, g_bback = mlp_grads(meta, n_dp, hiddens, gpres, mins, cotangent)
    out_away, out_kept = mlp_out(meta, hiddens, rest, full)

    def stacked_sum(own, sib):
        both = jnp.stack([own, sib], 1).reshape((n_dp,) + own.shape[1:])
        return lax.psum_scatter(both.astype(F32), "dp", scatter_dimension=0)

    def mp_sum(arr):
        return lax.psum(arr.astype(F32), "mp").astype(BF16)

    if not paired:
        for r in range(parts):
            totals[2 * r], totals[2 * r + 1] = mp_sum(keeps[r]), mp_sum(aways[r])
        out_sums = mp_sum(out_kept), mp_sum(out_away)
        grads = stacked_sum(own, sib)
    else:
        both = chip_sum(own, sib)
        grads = plane_sum(both, BF16)
        out_pair = add_low(out_kept, swapped(after(out_away, totals), 1))
        out_total = add_low(out_pair, swapped(out_pair, 2))
        out_sums = out_total, swapped(out_total, 1)
    hidden = w_in.shape[1]
    grad_in, grad_back = grads[:, :hidden], grads[:, hidden:].T

    def column(j):
        return bundles[j // per], j % per * 3 * (full // groups)

    gres, gmix, g_gain2 = norm_bwd(meta, totals, resids, cotangent, vec)
    acc, own, sib = attn_bwd(
        meta, n_dp, 0, column(0)[1], gmix, heads[0], rest, column(0)[0], (attn_in, *atts)
    )
    if paired:
        both = chip_sum(own, sib)
        gmix = after(gmix, both, out_pair)
        piece = plane_sum(both, BF16).astype(BF16)
        pieces = [piece] + [
            lax.ppermute(piece, "mp", [(i, (i + d) % 4) for i in range(4)]) for d in range(1, 4)
        ]
    else:
        every = lax.all_gather(stacked_sum(own, sib).astype(BF16), "mp")
        pieces = [every[d] for d in range(groups)]
    grad_qkv, grad_out = assemble(meta, groups, paired, pieces)
    for j in range(1, groups - 1):
        (acc,) = attn_bwd(
            meta, n_dp, j, column(j)[1], gmix, heads[j], rest, column(j)[0], (acc,)
        )
    j = groups - 1
    if paired:
        gmix = after(gmix, piece, out_total, grads)
    grad_tokens, own, sib = attn_bwd(
        meta, n_dp, j, column(j)[1], gmix, heads[j], rest, column(j)[0],
        (acc, tokens, gres, vec, g_gain2, g_bback, g_bin),
    )
    small = plane_sum(chip_sum(own, sib), F32) if paired else stacked_sum(own, sib)
    output = finish(meta, resids, *out_sums, vec)
    return (
        output, grad_tokens, grad_qkv, grad_out, small[0], small[1], grad_in,
        small[3, : b_in.shape[0]], grad_back, small[2],
    )


def solution(mesh):
    in_specs = (
        P("dp", None),
        P("dp"),
        P("dp", None),
        P("dp", None),
        P("dp"),
        P("dp"),
        P("dp", "mp"),
        P(("mp", "dp")),
        P("mp", "dp"),
        P("dp"),
        P("dp", None),
    )
    out_specs = (
        P("dp", None),
        P("dp", None),
        P("dp", None),
        P("dp", None),
        P("dp"),
        P("dp"),
        P("dp", "mp"),
        P(("mp", "dp")),
        P("mp", "dp"),
        P("dp"),
    )
    body = functools.partial(per_device, mesh.shape["dp"], mesh.shape["mp"])
    return jax.shard_map(
        body, mesh=mesh, in_specs=in_specs, out_specs=out_specs, check_vma=False
    )
```

profile of v0, /device:TPU:0, one launch (start us, length us, event | category | flops | bytes accessed | tf_op | source)
XLA Modules:
  0.0 309.4 jit_solution(11640505779067116569)
XLA Ops:
  12.5 7.0 %collective-permute-done.2.refs_2_.refs_21_.refs_17_ = bf16[144,1536]{1,0:T(8,128)(2,1)S(1)} collective-permute-done((bf16[144,1536]{1,0:T(8,128)(2,1)S(1)}, bf16[144,1536]{1,0:T(8,128)(2,1)S(1)}, u32[]{:S(2)}, u32[]{:S(2)}) %collective-permute-start.2) | collective-permute-done | bytes 442400 | tf_op jit(solution)/shard_map/ppermute | solution.py:892
  25.7 6.8 %collective-permute-done.6.refs_6_.refs_25_.refs_21_ = bf16[144,1536]{1,0:T(8,128)(2,1)S(1)} collective-permute-done((bf16[144,1536]{1,0:T(8,128)(2,1)S(1)}, bf16[144,1536]{1,0:T(8,128)(2,1)S(1)}, u32[]{:S(2)}, u32[]{:S(2)}) %collective-permute-start.6) | collective-permute-done | bytes 442400 | tf_op jit(solution)/shard_map/ppermute | solution.py:892
  33.0 5.5 %collective-permute-done.1.refs_2_.refs_17_.refs_23_ = bf16[128,1536]{1,0:T(8,128)(2,1)S(1)} collective-permute-done((bf16[128,1536]{1,0:T(8,128)(2,1)S(1)}, bf16[128,1536]{1,0:T(8,128)(2,1)S(1)}, u32[]{:S(2)}, u32[]{:S(2)}) %collective-permute-start.1) | collective-permute-done | bytes 393248 | tf_op jit(solution)/shard_map/ppermute | solution.py:892
  43.3 7.0 %attn_fwd.4 = (bf16[1024,256]{1,0:T(8,128)(2,1)S(1)}, bf16[1024,256]{1,0:T(8,128)(2,1)S(1)}, bf16[1024,256]{1,0:T(8,128)(2,1)S(1)}, bf16[1024,256]{1,0:T(8,128)(...) custom-call(s32[4]{0:T(128)S(1)} %pad_add_fusion.meta, ...), custom_call_target="tpu_custom_call" | custom-call | flops 8000000000 | bytes 6000000 | tf_op jit(solution)/shard_map/attn_fwd/pallas_call | solution.py:291
  53.4 5.6 %collective-permute-done.13.refs_6_.refs_21_.refs_27_ = bf16[128,1536]{1,0:T(8,128)(2,1)S(1)} collective-permute-done((bf16[128,1536]{1,0:T(8,128)(2,1)S(1)}, bf16[128,1536]{1,0:T(8,128)(2,1)S(1)}, u32[]{:S(2)}, u32[]{:S(2)}) %collective-permute-start.13) | collective-permute-done | bytes 393248 | tf_op jit(solution)/shard_map/ppermute | solution.py:892
  59.0 6.1 %attn_fwd.5 = (bf16[1024,256]{1,0:T(8,128)(2,1)S(1)}, bf16[1024,256]{1,0:T(8,128)(2,1)S(1)}, bf16[1024,256]{1,0:T(8,128)(2,1)S(1)}, bf16[1024,256]{1,0:T(8,128)(2,1)S(1)}, f32[1024,256]{1,0:T(8,128)S(1)}) custom-call(s32[4]{0:T(128)S(1)} %pad_add_fusion.meta, bf16[1024,1024]{1,0:T(8,128)(2,1)S(1)} %get-tuple-element.84.source.refs_6_, ...), custom_call_target="tpu_custom_call" | custom-call | flops 8000000000 | bytes 6000000 | tf_op jit(solution)/shard_map/attn_fwd/pallas_call | solution.py:291
  68.0 6.1 %attn_fwd.7 = (bf16[1024,256]{1,0:T(8,128)(2,1)S(1)}, bf16[1024,256]{1,0:T(8,128)(2,1)S(1)}, bf16[1024,256]{1,0:T(8,128)(2,1)S(1)}, bf16[1024,256]{1,0:T(8,128)(2,1)S(1)}, f32[1024,256]{1,0:T(8,128)S(1)}) custom-call(s32[4]{0:T(128)S(1)} %pad_add_fusion.meta, bf16[1024,1024]{1,0:T(8,128)(2,1)S(1)} %get-tuple-element.84.source.refs_6_, ...), custom_call_target="tpu_custom_call" | custom-call | flops 8000000000 | bytes 6000000 | tf_op jit(solution)/shard_map/attn_fwd/pallas_call | solution.py:291
  75.8 6.1 %attn_fwd.6 = (bf16[1024,256]{1,0:T(8,128)(2,1)S(1)}, bf16[1024,256]{1,0:T(8,128)(2,1)S(1)}, bf16[1024,256]{1,0:T(8,128)(2,1)S(1)}, bf16[1024,256]{1,0:T(8,128)(2,1)S(1)}, f32[1024,256]{1,0:T(8,128)S(1)}) custom-call(s32[4]{0:T(128)S(1)} %pad_add_fusion.meta, bf16[1024,1024]{1,0:T(8,128)(2,1)S(1)} %get-tuple-element.84.source.refs_6_, ...), custom_call_target="tpu_custom_call" | custom-call | flops 8000000000 | bytes 6000000 | tf_op jit(solution)/shard_map/attn_fwd/pallas_call | solution.py:291
  84.6 7.7 %mlp_fwd_bwd.3 = (bf16[256,1024]{1,0:T(8,128)(2,1)S(1)}, bf16[256,1024]{1,0:T(8,128)(2,1)S(1)}, bf16[512,1024]{1,0:T(8,128)(2,1)S(1)}, bf16[512,1024]{1,0:T(8,12...) custom-call(s32[4]{0:T(128)S(1)} %pad_add_fusion.meta, ...), custom_call_target="tpu_custom_call" | custom-call | flops 8000000000 | bytes 16000000 | tf_op jit(solution)/shard_map/mlp_fwd_bwd/pallas_call | solution.py:398
  94.0 7.9 %mlp_fwd_bwd.2 = (bf16[256,1024]{1,0:T(8,128)(2,1)S(1)}, bf16[256,1024]{1,0:T(8,128)(2,1)S(1)}, bf16[512,1024]{1,0:T(8,128)(2,1)S(1)}, bf16[512,1024]{1,0:T(8,12...) custom-call(s32[4]{0:T(128)S(1)} %pad_add_fusion.meta, ...), custom_call_target="tpu_custom_call" | custom-call | flops 8000000000 | bytes 16000000 | tf_op jit(solution)/shard_map/mlp_fwd_bwd/pallas_call | solution.py:398
  102.5 4.7 %collective-permute-done.24 = bf16[256,1024]{1,0:T(8,128)(2,1)S(1)} collective-permute-done((bf16[256,1024]{1,0:T(8,128)(2,1)S(1)}, bf16[256,1024]{1,0:T(8,128)(2,1)S(1)}, u32[]{:S(2)}, u32[]{:S(2)}) %collective-permute-start.24) | collective-permute-done | bytes 524320 | tf_op jit(solution)/shard_map/ppermute | solution.py:933
  110.0 17.8 %collective-permute-done.21 = bf16[256,1024]{1,0:T(8,128)(2,1)S(1)} collective-permute-done((bf16[256,1024]{1,0:T(8,128)(2,1)S(1)}, bf16[256,1024]{1,0:T(8,128)(2,1)S(1)}, u32[]{:S(2)}, u32[]{:S(2)}) %collective-permute-start.21) | collective-permute-done | bytes 524320 | tf_op jit(solution)/shard_map/ppermute | solution.py:933
  128.1 5.9 %mlp_grads.1 = (bf16[4,128,2048]{2,1,0:T(8,128)(2,1)S(1)}, bf16[4,128,2048]{2,1,0:T(8,128)(2,1)S(1)}, f32[1,1024]{1,0:T(1,128)S(1)}, f32[1,1024]{1,0:T(1,128)S(1)}) custom-call(s32[4]{0:T(128)S(1)} %pad_add_fusion.meta, bf16[512,1024]{1,0:T(8,128)(2,1)S(1)} %get-tuple-element.90.refs_0_, bf16[512,1024]{1,0:T(8,128)(2,1)S(1)} %get-tuple-element.91.refs_1_, ...), custom_call_target="tpu_custom_call" | custom-call | flops 8000000000 | bytes 16000000 | tf_op jit(solution)/shard_map/mlp_grads/pallas_call | solution.py:510
  134.1 11.1 %collective-permute-done.25 = bf16[256,1024]{1,0:T(8,128)(2,1)S(1)} collective-permute-done((bf16[256,1024]{1,0:T(8,128)(2,1)S(1)}, bf16[256,1024]{1,0:T(8,128)(2,1)S(1)}, u32[]{:S(2)}, u32[]{:S(2)}) %collective-permute-start.25) | collective-permute-done | bytes 524320 | tf_op jit(solution)/shard_map/ppermute | solution.py:933
  146.7 8.5 %collective-permute-done.22 = bf16[256,1024]{1,0:T(8,128)(2,1)S(1)} collective-permute-done((bf16[256,1024]{1,0:T(8,128)(2,1)S(1)}, bf16[256,1024]{1,0:T(8,128)(2,1)S(1)}, u32[]{:S(2)}, u32[]{:S(2)}) %collective-permute-start.22) | collective-permute-done | bytes 524320 | tf_op jit(solution)/shard_map/ppermute | solution.py:933
  159.5 6.9 %collective-permute-done.26.refs_3_ = bf16[256,1024]{1,0:T(8,128)(2,1)S(1)} collective-permute-done((bf16[256,1024]{1,0:T(8,128)(2,1)S(1)}, bf16[256,1024]{1,0:T(8,128)(2,1)S(1)}, u32[]{:S(2)}, u32[]{:S(2)}) %collective-permute-start.26) | collective-permute-done | bytes 524320 | tf_op jit(solution)/shard_map/ppermute | solution.py:933
  166.4 11.1 %collective-permute-done.23.refs_1_ = bf16[256,1024]{1,0:T(8,128)(2,1)S(1)} collective-permute-done((bf16[256,1024]{1,0:T(8,128)(2,1)S(1)}, bf16[256,1024]{1,0:T(8,128)(2,1)S(1)}, u32[]{:S(2)}, u32[]{:S(2)}) %collective-permute-start.23) | collective-permute-done | bytes 524320 | tf_op jit(solution)/shard_map/ppermute | solution.py:933
  182.3 14.2 %attn_bwd.4 = (f32[1024,1024]{1,0:T(8,128)S(1)}, bf16[4,128,1024]{2,1,0:T(8,128)(2,1)S(1)}, bf16[4,128,1024]{2,1,0:T(8,128)(2,1)S(1)}) custom-call(s32[4]{0:T(128)S(1)} %pad_add_fusion.meta, bf16[1024,1024]{1,0:T(8,128)(2,1)S(1)} %get-tuple-element.113.refs_0_, bf16[1024,256]{1,0:T(8,128)(2,1)S(1)} %copy-done.87, bf16[1024,256]{1,0:T(8,128)(2,1)S(1)} %copy-done.89, ...), custom_call_target="tpu_custom_call" | custom-call | flops 10000000000 | bytes 7000000 | tf_op jit(solution)/shard_map/attn_bwd/pallas_call | solution.py:823
  214.5 11.4 %attn_bwd.5.refs_6_ = f32[1024,1024]{1,0:T(8,128)S(1)} custom-call(s32[4]{0:T(128)S(1)} %pad_add_fusion.meta, bf16[1024,1024]{1,0:T(8,128)(2,1)S(1)} %get-tuple-element.113.refs_0_, bf16[1024,256]{1,0:T(8,128)(2,1)S(1)} %copy-done.67, bf16[1024,256]{1,0:T(8,128)(2,1)S(1)} %copy-done.69, bf16[1024,256]{1,0:T(8,128)(2,1)S(1)} %copy-done.71, ...), custom_call_target="tpu_custom_call" | custom-call | flops 10000000000 | bytes 7000000 | tf_op jit(solution)/shard_map/attn_bwd/pallas_call | solution.py:823
  226.0 11.2 %attn_bwd.6.refs_6_ = f32[1024,1024]{1,0:T(8,128)S(1)} custom-call(s32[4]{0:T(128)S(1)} %pad_add_fusion.meta, bf16[1024,1024]{1,0:T(8,128)(2,1)S(1)} %get-tuple-element.113.refs_0_, bf16[1024,256]{1,0:T(8,128)(2,1)S(1)} %copy-done.76, bf16[1024,256]{1,0:T(8,128)(2,1)S(1)} %copy-done.78, bf16[1024,256]{1,0:T(8,128)(2,1)S(1)} %copy-done.80, ...), custom_call_target="tpu_custom_call" | custom-call | flops 10000000000 | bytes 7000000 | tf_op jit(solution)/shard_map/attn_bwd/pallas_call | solution.py:823
  245.6 5.5 %collective-permute-done.32 = bf16[128,1024]{1,0:T(8,128)(2,1)S(1)} collective-permute-done((bf16[128,1024]{1,0:T(8,128)(2,1)S(1)}, bf16[128,1024]{1,0:T(8,128)(2,1)S(1)}, u32[]{:S(2)}, u32[]{:S(2)}) %collective-permute-start.32) | collective-permute-done | bytes 262176 | tf_op jit(solution)/shard_map/ppermute | solution.py:892
  257.8 11.6 %collective-permute-start.29 = (bf16[512,1024]{1,0:T(8,128)(2,1)S(1)}, bf16[512,1024]{1,0:T(8,128)(2,1)}, u32[]{:S(2)}, u32[]{:S(2)}) collective-permute-start(bf16[512,1024]{1,0:T(8,128)(2,1)S(1)} %add_convert_fusion.refs_2_), channel_id=1, source_target_pairs={{0,1},{1,0},{2,3},{3,2},{4,5},{5,4},{6,7},{7,6},{8,9},{9,8},{10,11... | collective-permute-start | bytes 3145736 | tf_op jit(solution)/shard_map/ppermute | solution.py:933
  269.4 13.8 %attn_bwd.7 = (f32[1024,1024]{1,0:T(8,128)}, f32[4,4,128]{2,1,0:T(4,128)S(1)}, f32[4,4,128]{2,1,0:T(4,128)S(1)}) custom-call(s32[4]{0:T(128)S(1)} %pad_add_fusion.meta, bf16[1024,1024]{1,0:T(8,128)(2,1)S(1)} %get-tuple-element.113.refs_0_, bf16[1024,256]{1,0:T(8,128)(2,1)S(1)} %copy-done.57, bf16[1024,256]{1,0:T(8,128)(2,1)S(1)} %copy-done.59, ...), custom_call_target="tpu_custom_call" | custom-call | flops 10000000000 | bytes 7000000 | tf_op jit(solution)/shard_map/attn_bwd/pallas_call | solution.py:823
  292.5 6.9 %collective-permute-done.38.refs_1_ = bf16[128,1024]{1,0:T(8,128)(2,1)} collective-permute-done((bf16[128,1024]{1,0:T(8,128)(2,1)S(1)}, bf16[128,1024]{1,0:T(8,128)(2,1)}, u32[]{:S(2)}, u32[]{:S(2)}) %collective-permute-start.38) | collective-permute-done | bytes 262176 | tf_op jit(solution)/shard_map/ppermute | solution.py:1038
  (292 shorter events, 100.5 us)
Async XLA Ops:
  21.8 19.4 %collective-permute-start.8 = (bf16[128,3072]{1,0:T(8,128)(2,1)S(1)}, bf16[128,3072]{1,0:T(8,128)(2,1)S(1)}, u32[]{:S(2)}, u32[]{:S(2)}) collective-permute-start(bf16[128,3072]{1,0:T(8,128)(2,1)S(1)} %get-tuple-element.83.refs_8_.refs_2_.refs_11_.refs_7_.refs_13_), channel_id=1, source_target_pairs={{0,8},{4,20},{8,0},{12,28},{16,24},{20,4},{24,16},{28,12},{1,9},{5... | collective-permute-start | bytes 2359304 | tf_op jit(solution)/shard_map/ppermute | solution.py:892
  39.8 27.7 %collective-permute-start.17 = (bf16[128,3072]{1,0:T(8,128)(2,1)S(1)}, bf16[128,3072]{1,0:T(8,128)(2,1)S(1)}, u32[]{:S(2)}, u32[]{:S(2)}) collective-permute-start(bf16[128,3072]{1,0:T(8,128)(2,1)S(1)} %get-tuple-element.83.refs_8_.refs_2_.refs_11_.refs_7_.refs_13_), channel_id=1, source_target_pairs={{0,16},{4,12},{8,24},{12,4},{16,0},{20,28},{24,8},{28,20},{1,17},{... | collective-permute-start | bytes 2359304 | tf_op jit(solution)/shard_map/ppermute | solution.py:892
  41.3 17.7 %collective-permute-start.13 = (bf16[128,1536]{1,0:T(8,128)(2,1)S(1)}, bf16[128,1536]{1,0:T(8,128)(2,1)S(1)}, u32[]{:S(2)}, u32[]{:S(2)}) collective-permute-start(bf16[128,1536]{1,0:T(8,128)(2,1)S(1)} %collective-permute-done.1.refs_2_.refs_17_.refs_23_), channel_id=1, source_target_pairs={{0,16},{4,12},{8,24},{12,4},{16,0},{20,28},{24,8},{28,20},{1,17},{... | collective-permute-start | bytes 1179656 | tf_op jit(solution)/shard_map/ppermute | solution.py:892
  41.8 26.1 %collective-permute-start.19 = (bf16[128,3072]{1,0:T(8,128)(2,1)S(1)}, bf16[128,3072]{1,0:T(8,128)(2,1)S(1)}, u32[]{:S(2)}, u32[]{:S(2)}) collective-permute-start(bf16[128,3072]{1,0:T(8,128)(2,1)S(1)} %collective-permute-done.8.refs_10_.refs_4_.refs_13_.refs_9_.refs_15_), channel_id=1, source_target_pairs={{0,16},{4,12},{8,24},{12,4},{16,0},{20,28},{24,8},{28,20},{1,17},{... | collective-permute-start | bytes 2359304 | tf_op jit(solution)/shard_map/ppermute | solution.py:892
  66.8 17.8 %collective-permute-start.15 = (bf16[128,3072]{1,0:T(8,128)(2,1)S(1)}, bf16[128,3072]{1,0:T(8,128)(2,1)S(1)}, u32[]{:S(2)}, u32[]{:S(2)}) collective-permute-start(bf16[128,3072]{1,0:T(8,128)(2,1)S(1)} %get-tuple-element.83.refs_8_.refs_2_.refs_11_.refs_7_.refs_13_), channel_id=1, source_target_pairs={{0,4},{4,0},{8,12},{12,8},{16,20},{20,16},{24,28},{28,24},{1,5},{5... | collective-permute-start | bytes 2359304 | tf_op jit(solution)/shard_map/ppermute | solution.py:892
  67.4 17.3 %collective-permute-start.16 = (bf16[128,3072]{1,0:T(8,128)(2,1)S(1)}, bf16[128,3072]{1,0:T(8,128)(2,1)S(1)}, u32[]{:S(2)}, u32[]{:S(2)}) collective-permute-start(bf16[128,3072]{1,0:T(8,128)(2,1)S(1)} %collective-permute-done.8.refs_10_.refs_4_.refs_13_.refs_9_.refs_15_), channel_id=1, source_target_pairs={{0,4},{4,0},{8,12},{12,8},{16,20},{20,16},{24,28},{28,24},{1,5},{5... | collective-permute-start | bytes 2359304 | tf_op jit(solution)/shard_map/ppermute | solution.py:892
  67.5 17.2 %collective-permute-start.18 = (bf16[128,3072]{1,0:T(8,128)(2,1)S(1)}, bf16[128,3072]{1,0:T(8,128)(2,1)S(1)}, u32[]{:S(2)}, u32[]{:S(2)}) collective-permute-start(bf16[128,3072]{1,0:T(8,128)(2,1)S(1)} %collective-permute-done.17.refs_12_.refs_6_.refs_15_.refs_11_.refs_17_), channel_id=1, source_target_pairs={{0,4},{4,0},{8,12},{12,8},{16,20},{20,16},{24,28},{28,24},{1,5},{5... | collective-permute-start | bytes 2359304 | tf_op jit(solution)/shard_map/ppermute | solution.py:892
  67.9 16.8 %collective-permute-start.20 = (bf16[128,3072]{1,0:T(8,128)(2,1)S(1)}, bf16[128,3072]{1,0:T(8,128)(2,1)S(1)}, u32[]{:S(2)}, u32[]{:S(2)}) collective-permute-start(bf16[128,3072]{1,0:T(8,128)(2,1)S(1)} %collective-permute-done.19.refs_14_.refs_8_.refs_17_.refs_13_.refs_19_), channel_id=1, source_target_pairs={{0,4},{4,0},{8,12},{12,8},{16,20},{20,16},{24,28},{28,24},{1,5},{5... | collective-permute-start | bytes 2359304 | tf_op jit(solution)/shard_map/ppermute | solution.py:892
  101.9 25.9 %collective-permute-start.21 = (bf16[256,1024]{1,0:T(8,128)(2,1)S(1)}, bf16[256,1024]{1,0:T(8,128)(2,1)S(1)}, u32[]{:S(2)}, u32[]{:S(2)}) collective-permute-start(bf16[256,1024]{1,0:T(8,128)(2,1)S(1)} %get-tuple-element.95), channel_id=1, source_target_pairs={{0,1},{1,0},{2,3},{3,2},{4,5},{5,4},{6,7},{7,6},{8,9},{9,8},{10,11... | collective-permute-start | bytes 1572872 | tf_op jit(solution)/shard_map/ppermute | solution.py:933
  107.3 37.8 %collective-permute-start.25 = (bf16[256,1024]{1,0:T(8,128)(2,1)S(1)}, bf16[256,1024]{1,0:T(8,128)(2,1)S(1)}, u32[]{:S(2)}, u32[]{:S(2)}) collective-permute-start(bf16[256,1024]{1,0:T(8,128)(2,1)S(1)} %add_convert_fusion.3), channel_id=1, source_target_pairs={{0,2},{1,3},{2,0},{3,1},{4,6},{5,7},{6,4},{7,5},{8,10},{9,11},{10,... | collective-permute-start | bytes 1572872 | tf_op jit(solution)/shard_map/ppermute | solution.py:933
  128.0 27.1 %collective-permute-start.22 = (bf16[256,1024]{1,0:T(8,128)(2,1)S(1)}, bf16[256,1024]{1,0:T(8,128)(2,1)S(1)}, u32[]{:S(2)}, u32[]{:S(2)}) collective-permute-start(bf16[256,1024]{1,0:T(8,128)(2,1)S(1)} %add_convert_fusion.5), channel_id=1, source_target_pairs={{0,2},{1,3},{2,0},{3,1},{4,6},{5,7},{6,4},{7,5},{8,10},{9,11},{10,... | collective-permute-start | bytes 1572872 | tf_op jit(solution)/shard_map/ppermute | solution.py:933
  134.0 62.6 %collective-permute-start.34 = (bf16[4,128,2048]{2,1,0:T(8,128)(2,1)S(1)}, bf16[4,128,2048]{2,1,0:T(8,128)(2,1)}, u32[]{:S(2)}, u32[]{:S(2)}) collective-permute-start(bf16[4,128,2048]{2,1,0:T(8,128)(2,1)S(1)} %get-tuple-element.112), channel_id=1, source_target_pairs={{0,4},{4,0},{8,12},{12,8},{16,20},{20,16},{24,28},{28,24},{1,5},{5... | collective-permute-start | bytes 6291464 | tf_op jit(solution)/shard_map/ppermute | solution.py:892
  145.4 21.0 %collective-permute-start.26 = (bf16[256,1024]{1,0:T(8,128)(2,1)S(1)}, bf16[256,1024]{1,0:T(8,128)(2,1)S(1)}, u32[]{:S(2)}, u32[]{:S(2)}) collective-permute-start(bf16[256,1024]{1,0:T(8,128)(2,1)S(1)} %add_convert_fusion.2.refs_2_), channel_id=1, source_target_pairs={{0,1},{1,0},{2,3},{3,2},{4,5},{5,4},{6,7},{7,6},{8,9},{9,8},{10,11... | collective-permute-start | bytes 1572872 | tf_op jit(solution)/shard_map/ppermute | solution.py:933
  155.4 22.2 %collective-permute-start.23 = (bf16[256,1024]{1,0:T(8,128)(2,1)S(1)}, bf16[256,1024]{1,0:T(8,128)(2,1)S(1)}, u32[]{:S(2)}, u32[]{:S(2)}) collective-permute-start(bf16[256,1024]{1,0:T(8,128)(2,1)S(1)} %add_convert_fusion.4.refs_0_), channel_id=1, source_target_pairs={{0,1},{1,0},{2,3},{3,2},{4,5},{5,4},{6,7},{7,6},{8,9},{9,8},{10,11... | collective-permute-start | bytes 1572872 | tf_op jit(solution)/shard_map/ppermute | solution.py:933
  177.5 28.3 %collective-permute-start.27 = (bf16[512,1024]{1,0:T(8,128)(2,1)S(1)}, bf16[512,1024]{1,0:T(8,128)(2,1)}, u32[]{:S(2)}, u32[]{:S(2)}) collective-permute-start(bf16[512,1024]{1,0:T(8,128)(2,1)S(1)} %get-tuple-element.98), channel_id=1, source_target_pairs={{0,1},{1,0},{2,3},{3,2},{4,5},{5,4},{6,7},{7,6},{8,9},{9,8},{10,11... | collective-permute-start | bytes 3145736 | tf_op jit(solution)/shard_map/ppermute | solution.py:933
  202.3 34.9 %collective-permute-start.35 = (bf16[128,2048]{1,0:T(8,128)(2,1)}, bf16[128,2048]{1,0:T(8,128)(2,1)S(1)}, u32[]{:S(2)}, u32[]{:S(2)}) collective-permute-start(bf16[128,2048]{1,0:T(8,128)(2,1)} %get-tuple-element.148), channel_id=1, source_target_pairs={{0,8},{4,12},{8,0},{12,4},{16,24},{20,28},{24,16},{28,20},{1,9},{5... | collective-permute-start | bytes 1572872 | tf_op jit(solution)/shard_map/ppermute | solution.py:892
  204.3 34.2 %collective-permute-start.37 = (bf16[128,2048]{1,0:T(8,128)(2,1)}, bf16[128,2048]{1,0:T(8,128)(2,1)}, u32[]{:S(2)}, u32[]{:S(2)}) collective-permute-start(bf16[128,2048]{1,0:T(8,128)(2,1)} %get-tuple-element.149), channel_id=1, source_target_pairs={{0,24},{4,28},{8,16},{12,20},{16,8},{20,12},{24,0},{28,4},{1,25},{... | collective-permute-start | bytes 1572872 | tf_op jit(solution)/shard_map/ppermute | solution.py:892
  204.8 35.4 %collective-permute-start.36 = (bf16[128,2048]{1,0:T(8,128)(2,1)}, bf16[128,2048]{1,0:T(8,128)(2,1)}, u32[]{:S(2)}, u32[]{:S(2)}) collective-permute-start(bf16[128,2048]{1,0:T(8,128)(2,1)} %get-tuple-element.150), channel_id=1, source_target_pairs={{0,16},{4,20},{8,24},{12,28},{16,0},{20,4},{24,8},{28,12},{1,17},{... | collective-permute-start | bytes 1572872 | tf_op jit(solution)/shard_map/ppermute | solution.py:892
  207.4 50.0 %collective-permute-start.28 = (bf16[512,1024]{1,0:T(8,128)(2,1)S(1)}, bf16[512,1024]{1,0:T(8,128)(2,1)S(1)}, u32[]{:S(2)}, u32[]{:S(2)}) collective-permute-start(bf16[512,1024]{1,0:T(8,128)(2,1)S(1)} %add_convert_fusion.1), channel_id=1, source_target_pairs={{0,2},{1,3},{2,0},{3,1},{4,6},{5,7},{6,4},{7,5},{8,10},{9,11},{10,... | collective-permute-start | bytes 3145736 | tf_op jit(solution)/shard_map/ppermute | solution.py:933
  212.2 29.8 %collective-permute-start.31 = (bf16[128,1024]{1,0:T(8,128)(2,1)S(1)}, bf16[128,1024]{1,0:T(8,128)(2,1)S(1)}, u32[]{:S(2)}, u32[]{:S(2)}) collective-permute-start(bf16[128,1024]{1,0:T(8,128)(2,1)S(1)} %get-tuple-element.155), channel_id=1, source_target_pairs={{0,8},{4,12},{8,0},{12,4},{16,24},{20,28},{24,16},{28,20},{1,9},{5... | collective-permute-start | bytes 786440 | tf_op jit(solution)/shard_map/ppermute | solution.py:892
  251.2 35.3 %collective-permute-start.40 = (bf16[128,1024]{1,0:T(8,128)(2,1)S(1)}, bf16[128,1024]{1,0:T(8,128)(2,1)S(1)}, u32[]{:S(2)}, u32[]{:S(2)}) collective-permute-start(bf16[128,1024]{1,0:T(8,128)(2,1)S(1)} %fusion.9.refs_0_), channel_id=1, source_target_pairs={{0,3},{1,0},{2,1},{3,2},{4,7},{5,4},{6,5},{7,6},{8,11},{9,8},{10,9... | collective-permute-start | bytes 786440 | tf_op jit(solution)/shard_map/ppermute | solution.py:1038
  251.5 36.2 %collective-permute-start.39 = (bf16[128,1024]{1,0:T(8,128)(2,1)S(1)}, bf16[128,1024]{1,0:T(8,128)(2,1)S(1)}, u32[]{:S(2)}, u32[]{:S(2)}) collective-permute-start(bf16[128,1024]{1,0:T(8,128)(2,1)S(1)} %fusion.9.refs_0_), channel_id=1, source_target_pairs={{0,2},{1,3},{2,0},{3,1},{4,6},{5,7},{6,4},{7,5},{8,10},{9,11},{10,... | collective-permute-start | bytes 786440 | tf_op jit(solution)/shard_map/ppermute | solution.py:1038
  257.8 46.5 %collective-permute-start.29 = (bf16[512,1024]{1,0:T(8,128)(2,1)S(1)}, bf16[512,1024]{1,0:T(8,128)(2,1)}, u32[]{:S(2)}, u32[]{:S(2)}) collective-permute-start(bf16[512,1024]{1,0:T(8,128)(2,1)S(1)} %add_convert_fusion.refs_2_), channel_id=1, source_target_pairs={{0,1},{1,0},{2,3},{3,2},{4,5},{5,4},{6,7},{7,6},{8,9},{9,8},{10,11... | collective-permute-start | bytes 3145736 | tf_op jit(solution)/shard_map/ppermute | solution.py:933
  284.5 19.3 %collective-permute-start.42 = (f32[4,128]{1,0:T(4,128)S(1)}, f32[4,128]{1,0:T(4,128)S(1)}, u32[]{:S(2)}, u32[]{:S(2)}) collective-permute-start(f32[4,128]{1,0:T(4,128)S(1)} %get-tuple-element.158), channel_id=1, source_target_pairs={{0,8},{4,12},{8,0},{12,4},{16,24},{20,28},{24,16},{28,20},{1,9},{5... | collective-permute-start | bytes 6152 | tf_op jit(solution)/shard_map/ppermute | solution.py:892
  (113 other events, 1431.7 us)
where the time goes:
time: 313 us; the launch traced here: 309 us
  Pallas kernels  112 us (36%)
  waiting for transfers between devices  107 us (34%)
  starting transfers between devices  52.5 us (17%)
  local copies, waits for them, and re-layouts  22.4 us (7%)
  other arithmetic  12.9 us (4%)
    ppermute x9, waiting for transfers between devices, swapped(): return lax.ppermute(arr, 'mp', [(i, i ^ bits) for i in range(4)])  64.8 us
    pallas_call x4, Pallas kernels, attn_bwd(): pl.pallas_call(functools.partial(attn_bwd_kernel, shape), grid=(count,),...  50.4 us
    ppermute x33, waiting for transfers between devices, send(): return lax.ppermute(arr, 'dp', [(i, move(i)) for i in range(PAIRED)])  35.1 us
    ppermute x33, starting transfers between devices, send(): return lax.ppermute(arr, 'dp', [(i, move(i)) for i in range(PAIRED)])  28.1 us
    pallas_call x4, Pallas kernels, attn_fwd(): pl.pallas_call(functools.partial(attn_fwd_kernel, n, count_vec, position...  25.3 us
    ppermute x9, starting transfers between devices, swapped(): return lax.ppermute(arr, 'mp', [(i, i ^ bits) for i in range(4)])  22.8 us
    unnamed x185, local copies, waits for them, and re-layouts  19.5 us
    pallas_call x2, Pallas kernels, mlp(): pl.pallas_call(functools.partial(mlp_kernel, n, n_atts, groups, part), ou...  15.6 us
  transfers between devices with their start and end apart: 45, of which 15 were waited for; matrix products, arithmetic and copies ran while one was open for 6% of the time, Pallas kernels for 32%

commit v1 on v0

--- a/solution.py
+++ b/solution.py
@@ -196,26 +196,24 @@
     fq_out, fk_out, val_out, att_out, rden_out = refs[n_pieces : n_pieces + 5]
     rest = refs[n_pieces + 5 :]
     if count_vec:
-        attn_in, vec_out, weight, states, sems, vec_scr, vec_sems = rest
+        attn_in, vec_out, weight, sems, vec_scr, vec_sems = rest
     else:
-        weight, states, sems = rest
+        weight, sems = rest
         attn_in = source
     width = fq_out.shape[1]
     pairs = width // PAIR
-
-    @pl.when(pl.program_id(0) == 0)
-    def _():
-        copies = piece_copies(meta[0], pieces, weight, sems, None, (start, 3 * width))
-        moves = []
-        if count_vec:
-            size = vec_out.shape[1] // n_pieces
-            moves = [
-                pltpu.make_async_copy(
-                    piece.at[pl.ds(size, vec_scr.shape[1])], vec_scr.at[k], vec_sems.at[k]
-                )
-                for k, piece in enumerate(pieces)
-            ]
-        start_all(moves + copies)
+    copies = piece_copies(meta[0], pieces, weight, sems, None, (start, 3 * width))
+    count = source.shape[0] // CHUNK
+    if count_vec:
+        size = vec_out.shape[1] // n_pieces
+        moves = [
+            pltpu.make_async_copy(
+                piece.at[pl.ds(size, vec_scr.shape[1])], vec_scr.at[k], vec_sems.at[k]
+            )
+            for k, piece in enumerate(pieces)
+        ]
+        start_all(moves)
+        start_all(copies)
         for k, move in enumerate(moves):
             move.wait()
             value = vec_scr[k].astype(F32)[0:1]
@@ -226,63 +224,64 @@
                     for t in range(3)
                 ]
                 vec_out[a : a + 1, at] = parts[0] + parts[1] + parts[2]
-        states[...] = jnp.zeros_like(states)
-        wait_all(copies)
-
-    if count_vec:
-        attn_in[...] = (source[...] * vec_out[0:1, :]).astype(BF16)
+        gain = vec_out[0:1, :]
+        for c in range(count):
+            rows = pl.ds(c * CHUNK, CHUNK)
+            attn_in[rows, :] = (source[rows, :] * gain).astype(BF16)
+    else:
+        start_all(copies)
+    wait_all(copies)
     mask_a, mask_b = lane_masks()
     blocks = block_mask()
     first = lax.broadcasted_iota(jnp.int32, (CHUNK, PAIR), 1) < HD
     causal = lax.broadcasted_iota(jnp.int32, (CHUNK, CHUNK), 0) >= lax.broadcasted_iota(
         jnp.int32, (CHUNK, CHUNK), 1
     )
-    proj = nn(attn_in[...], weight[...])
-    query, keys = proj[:, :width], proj[:, width : 2 * width]
-    fq = jnp.where(query > 0, query + 1.0, jnp.exp(jnp.minimum(query, 0.0))).astype(BF16)
-    fk = jnp.where(keys > 0, keys + 1.0, jnp.exp(jnp.minimum(keys, 0.0))).astype(BF16)
-    val = proj[:, 2 * width :].astype(BF16)
-    fq_out[...] = fq
-    fk_out[...] = fk
-    val_out[...] = val
-    for p in range(pairs):
-        q, k, v = pair_of(fq, p), pair_of(fk, p), pair_of(val, p)
-        v_a = v * mask_a + mask_b
-        v_b = v * mask_b + mask_a
-        s_a = jnp.where(causal, nt(q * mask_a, k), 0.0).astype(BF16)
-        s_b = jnp.where(causal, nt(q * mask_b, k), 0.0).astype(BF16)
-        high, low = split(states[p])
-        past = nn(q, high) + nn(q, low)
-        r_a = nn(s_a, v_a) + past[:, :PAIR]
-        r_b = nn(s_b, v_b) + past[:, PAIR:]
-        numer = jnp.where(first, r_a, r_b)
-        denom = pltpu.roll(jnp.where(first, r_b, r_a), HD, axis=1)
-        inverse = 1.0 / denom
-        cols = pl.ds(p * PAIR, PAIR)
-        att_out[:, cols] = (numer * inverse).astype(BF16)
-        rden_out[:, cols] = inverse
-        states[p] = states[p] + tn(k, jnp.concatenate([v_a, v_b], 1)) * blocks
+    states = [None] * pairs
+    for c in range(count):
+        rows = pl.ds(c * CHUNK, CHUNK)
+        proj = nn(attn_in[rows, :], weight[...])
+        query, keys = proj[:, :width], proj[:, width : 2 * width]
+        fq = jnp.where(query > 0, query + 1.0, jnp.exp(jnp.minimum(query, 0.0))).astype(BF16)
+        fk = jnp.where(keys > 0, keys + 1.0, jnp.exp(jnp.minimum(keys, 0.0))).astype(BF16)
+        val = proj[:, 2 * width :].astype(BF16)
+        fq_out[rows, :] = fq
+        fk_out[rows, :] = fk
+        val_out[rows, :] = val
+        for p in range(pairs):
+            q, k, v = pair_of(fq, p), pair_of(fk, p), pair_of(val, p)
+            v_a = v * mask_a + mask_b
+            v_b = v * mask_b + mask_a
+            s_a = jnp.where(causal, nt(q * mask_a, k), 0.0).astype(BF16)
+            s_b = jnp.where(causal, nt(q * mask_b, k), 0.0).astype(BF16)
+            r_a, r_b = nn(s_a, v_a), nn(s_b, v_b)
+            if c > 0:
+                high, low = split(states[p])
+                past = nn(q, high) + nn(q, low)
+                r_a = r_a + past[:, :PAIR]
+                r_b = r_b + past[:, PAIR:]
+            numer = jnp.where(first, r_a, r_b)
+            denom = pltpu.roll(jnp.where(first, r_b, r_a), HD, axis=1)
+            inverse = 1.0 / denom
+            cols = pl.ds(p * PAIR, PAIR)
+            att_out[rows, cols] = (numer * inverse).astype(BF16)
+            rden_out[rows, cols] = inverse.astype(BF16)
+            if c + 1 < count:
+                new = tn(k, jnp.concatenate([v_a, v_b], 1)) * blocks
+                states[p] = new if c == 0 else states[p] + new
 
 
 def attn_fwd(meta, source, pieces, groups, position, count_vec):
     rows, full = source.shape
     width = full // groups
     n = len(pieces)
-    low = jax.ShapeDtypeStruct((rows, width), BF16)
-    shapes = [low, low, low, low, jax.ShapeDtypeStruct((rows, width), F32)]
-    specs = [pl.BlockSpec((CHUNK, width), lambda i: (i, 0))] * 5
-    wide = pl.BlockSpec((CHUNK, full), lambda i: (i, 0))
-    scratch = [
-        pltpu.VMEM((full, 3 * width), BF16),
-        pltpu.VMEM((width // PAIR, PAIR, 2 * PAIR), F32),
-        pltpu.SemaphoreType.DMA((n,)),
-    ]
+    shapes = [jax.ShapeDtypeStruct((rows, width), BF16)] * 5
+    scratch = [pltpu.VMEM((full, 3 * width), BF16), pltpu.SemaphoreType.DMA((n,))]
     if count_vec:
         shapes += [
             jax.ShapeDtypeStruct((rows, full), BF16),
             jax.ShapeDtypeStruct((count_vec, full), F32),
         ]
-        specs += [wide, pl.BlockSpec((count_vec, full), lambda i: (0, 0))]
         vec_rows = pieces[0].shape[0] - full // n
         scratch += [
             pltpu.VMEM((n, vec_rows, pieces[0].shape[1]), BF16),
@@ -290,10 +289,9 @@
         ]
     return pl.pallas_call(
         functools.partial(attn_fwd_kernel, n, count_vec, position * 3 * width),
-        grid=(rows // CHUNK,),
         out_shape=tuple(shapes),
-        in_specs=[SMEM, wide] + [ANY] * n,
-        out_specs=tuple(specs),
+        in_specs=[SMEM, VMEM] + [ANY] * n,
+        out_specs=(VMEM,) * len(shapes),
         scratch_shapes=scratch,
         compiler_params=pltpu.CompilerParams(vmem_limit_bytes=VMEM_LIMIT),
         cost_estimate=cost(8, 6),
@@ -695,7 +693,7 @@
     head_sum = (head_row == head_col).astype(F32).astype(BF16)
     rows = pl.ds(pl.multiple_of(c * CHUNK, CHUNK), CHUNK)
     grad_att = nt(gmix[...], w_o[...])
-    inverse = rden[...]
+    inverse = rden[...].astype(F32)
     gnum = (grad_att * inverse).astype(BF16)
     dots = nn((grad_att * att[...].astype(F32)).astype(BF16), head_sum)
     gden = (-dots * inverse).astype(BF16).astype(F32)
@@ -864,7 +862,7 @@
     pieces, (qkv, out) = refs[:-2], refs[-2:]
     width = out.shape[1] // groups
     for d, piece in enumerate(pieces):
-        group = lax.rem(meta[1] - d + groups, groups) if turned else d
+        group = meta[1] ^ d if turned else d
         for t in range(4):
             value = piece[:, pl.ds(t * width, width)].astype(F32)
             start = t % 3 * groups * width + group * width
@@ -999,7 +997,7 @@
         for r in reversed(range(parts)):
             totals[2 * r] = add_low(pairs[r], swapped(pairs[r], 2))
             totals[2 * r + 1] = swapped(totals[2 * r], 1)
-    own, sib, g_bin, g_bback = mlp_grads(meta, n_dp, hiddens, gpres, mins, cotangent)
+    wide_own, wide_sib, g_bin, g_bback = mlp_grads(meta, n_dp, hiddens, gpres, mins, cotangent)
     out_away, out_kept = mlp_out(meta, hiddens, rest, full)
 
     def stacked_sum(own, sib):
@@ -1013,15 +1011,11 @@
         for r in range(parts):
             totals[2 * r], totals[2 * r + 1] = mp_sum(keeps[r]), mp_sum(aways[r])
         out_sums = mp_sum(out_kept), mp_sum(out_away)
-        grads = stacked_sum(own, sib)
+        grads = stacked_sum(wide_own, wide_sib)
     else:
-        both = chip_sum(own, sib)
-        grads = plane_sum(both, BF16)
-        out_pair = add_low(out_kept, swapped(after(out_away, totals), 1))
-        out_total = add_low(out_pair, swapped(out_pair, 2))
-        out_sums = out_total, swapped(out_total, 1)
-    hidden = w_in.shape[1]
-    grad_in, grad_back = grads[:, :hidden], grads[:, hidden:].T
+        out_pair = add_low(out_kept, swapped(after(out_away, pairs[0]), 1))
+        totals = after(totals, out_pair)
+        got = send(wide_sib, across)
 
     def column(j):
         return bundles[j // per], j % per * 3 * (full // groups)
@@ -1031,29 +1025,42 @@
         meta, n_dp, 0, column(0)[1], gmix, heads[0], rest, column(0)[0], (attn_in, *atts)
     )
     if paired:
-        both = chip_sum(own, sib)
-        gmix = after(gmix, both, out_pair)
+        out_total = add_low(out_pair, swapped(out_pair, 2))
+        both = chip_sum(own, after(sib, out_total))
+        gmix = after(gmix, both)
         piece = plane_sum(both, BF16).astype(BF16)
-        pieces = [piece] + [
-            lax.ppermute(piece, "mp", [(i, (i + d) % 4) for i in range(4)]) for d in range(1, 4)
-        ]
+        out_sums = out_total, swapped(out_total, 1)
+        second = swapped(piece, 2)
+        pieces = [piece, swapped(piece, 1), second, swapped(second, 1)]
+        away = after(add_low(wide_own[1::2], got[1::2]), piece)
+        kept = wide_own[::2].astype(F32) + got[::2].astype(F32)
+        kept = kept + send(away, lambda i: i ^ 2).astype(F32)
+        low = after(kept[1].astype(BF16), second)
+        grads = kept[0] + send(low, lambda i: i ^ 4).astype(F32)
     else:
         every = lax.all_gather(stacked_sum(own, sib).astype(BF16), "mp")
         pieces = [every[d] for d in range(groups)]
     grad_qkv, grad_out = assemble(meta, groups, paired, pieces)
     for j in range(1, groups - 1):
+        if paired and j == groups - 2:
+            gmix = after(gmix, piece, out_total)
         (acc,) = attn_bwd(
             meta, n_dp, j, column(j)[1], gmix, heads[j], rest, column(j)[0], (acc,)
         )
     j = groups - 1
     if paired:
-        gmix = after(gmix, piece, out_total, grads)
+        gmix = after(gmix, second)
     grad_tokens, own, sib = attn_bwd(
         meta, n_dp, j, column(j)[1], gmix, heads[j], rest, column(j)[0],
         (acc, tokens, gres, vec, g_gain2, g_bback, g_bin),
     )
-    small = plane_sum(chip_sum(own, sib), F32) if paired else stacked_sum(own, sib)
-    output = finish(meta, resids, *out_sums, vec)
+    if paired:
+        small = plane_sum(chip_sum(own, after(sib, out_sums, pieces)), F32)
+    else:
+        small = stacked_sum(own, sib)
+    output = finish(meta, resids, *out_sums, after(vec, acc))
+    hidden = w_in.shape[1]
+    grad_in, grad_back = grads[:, :hidden], grads[:, hidden:].T
     return (
         output, grad_tokens, grad_qkv, grad_out, small[0], small[1], grad_in,
         small[3, : b_in.shape[0]], grad_back, small[2],

time: 313 us -> 298 us (0.952)
  starting transfers between devices: 52.5 us -> 41.2 us
  waiting for transfers between devices: 107 us -> 118 us
  local copies, waits for them, and re-layouts: 22.4 us -> 15.1 us
  Pallas kernels: 112 us -> 108 us
    ppermute x9 -> x12, waiting for transfers between devices: 64.8 us -> 84.7 us  [swapped(): return lax.ppermute(arr, 'mp', [(i, i ^ bits) for i in range(4)])]
    ppermute x9 -> x12, starting transfers between devices: 22.8 us -> 15.7 us  [swapped(): return lax.ppermute(arr, 'mp', [(i, i ^ bits) for i in range(4)])]
    ppermute x3 -> x0, waiting for transfers between devices: 6.88 us -> none  [per_device(): lax.ppermute(piece, 'mp', [(i, (i + d) % 4) for i in range(4)])]
    unnamed x185 -> x163, local copies, waits for them, and re-layouts: 19.5 us -> 13.5 us
    another operation x2 -> x1, other arithmetic: 4.99 us -> 0.47 us
    ppermute x33 -> x32, starting transfers between devices: 28.1 us -> 25.5 us  [send(): return lax.ppermute(arr, 'dp', [(i, move(i)) for i in range(PAIRED)])]
    ppermute x33 -> x32, waiting for transfers between devices: 35.1 us -> 33.1 us  [send(): return lax.ppermute(arr, 'dp', [(i, move(i)) for i in range(PAIRED)])]
  transfers between devices with their start and end apart: 45 -> 44, of which waited for: 15 -> 14; matrix products, arithmetic and copies ran while one was open for 6% -> 3% of each run, Pallas kernels for 32% -> 34%
where the time goes in v1:
time: 298 us; the launch traced here: 295 us
  waiting for transfers between devices  118 us (40%)
  Pallas kernels  108 us (36%)
  starting transfers between devices  41.2 us (14%)
  local copies, waits for them, and re-layouts  15.1 us (5%)
  other arithmetic  9.84 us (3%)
    ppermute x12, waiting for transfers between devices, swapped(): return lax.ppermute(arr, 'mp', [(i, i ^ bits) for i in range(4)])  84.7 us
    pallas_call x4, Pallas kernels, attn_bwd(): pl.pallas_call(functools.partial(attn_bwd_kernel, shape), grid=(count,),...  50.5 us
    ppermute x32, waiting for transfers between devices, send(): return lax.ppermute(arr, 'dp', [(i, move(i)) for i in range(PAIRED)])  33.1 us
    ppermute x32, starting transfers between devices, send(): return lax.ppermute(arr, 'dp', [(i, move(i)) for i in range(PAIRED)])  25.5 us
    pallas_call x4, Pallas kernels, attn_fwd(): pl.pallas_call(functools.partial(attn_fwd_kernel, n, count_vec, position...  22.5 us
    ppermute x12, starting transfers between devices, swapped(): return lax.ppermute(arr, 'mp', [(i, i ^ bits) for i in range(4)])  15.7 us
    pallas_call x2, Pallas kernels, mlp(): pl.pallas_call(functools.partial(mlp_kernel, n, n_atts, groups, part), ou...  15.6 us
    unnamed x163, local copies, waits for them, and re-layouts  13.5 us
  transfers between devices with their start and end apart: 44, of which 14 were waited for; matrix products, arithmetic and copies ran while one was open for 3% of the time, Pallas kernels for 34%

profile of v1, /device:TPU:0, one launch (start us, length us, event | category | flops | bytes accessed | tf_op | source)
XLA Modules:
  0.0 294.8 jit_solution(14338189210650113502)
XLA Ops:
  12.5 7.0 %collective-permute-done.2.refs_2_.refs_21_.refs_17_ = bf16[144,1536]{1,0:T(8,128)(2,1)S(1)} collective-permute-done((bf16[144,1536]{1,0:T(8,128)(2,1)S(1)}, bf16[144,1536]{1,0:T(8,128)(2,1)S(1)}, u32[]{:S(2)}, u32[]{:S(2)}) %collective-permute-start.2) | collective-permute-done | bytes 442400 | tf_op jit(solution)/shard_map/ppermute | solution.py:890
  25.7 6.8 %collective-permute-done.6.refs_6_.refs_25_.refs_21_ = bf16[144,1536]{1,0:T(8,128)(2,1)S(1)} collective-permute-done((bf16[144,1536]{1,0:T(8,128)(2,1)S(1)}, bf16[144,1536]{1,0:T(8,128)(2,1)S(1)}, u32[]{:S(2)}, u32[]{:S(2)}) %collective-permute-start.6) | collective-permute-done | bytes 442400 | tf_op jit(solution)/shard_map/ppermute | solution.py:890
  33.0 5.5 %collective-permute-done.1.refs_2_.refs_17_.refs_23_ = bf16[128,1536]{1,0:T(8,128)(2,1)S(1)} collective-permute-done((bf16[128,1536]{1,0:T(8,128)(2,1)S(1)}, bf16[128,1536]{1,0:T(8,128)(2,1)S(1)}, u32[]{:S(2)}, u32[]{:S(2)}) %collective-permute-start.1) | collective-permute-done | bytes 393248 | tf_op jit(solution)/shard_map/ppermute | solution.py:890
  43.3 6.7 %attn_fwd.4 = (bf16[1024,256]{1,0:T(8,128)(2,1)S(1)}, bf16[1024,256]{1,0:T(8,128)(2,1)S(1)}, bf16[1024,256]{1,0:T(8,128)(2,1)S(1)}, bf16[1024,256]{1,0:T(8,128)(...) custom-call(s32[4]{0:T(128)S(1)} %pad_add_fusion.meta, ...), custom_call_target="tpu_custom_call" | custom-call | flops 8000000000 | bytes 6000000 | tf_op jit(solution)/shard_map/attn_fwd/pallas_call | solution.py:290
  52.3 6.7 %collective-permute-done.13.refs_6_.refs_21_.refs_27_ = bf16[128,1536]{1,0:T(8,128)(2,1)S(1)} collective-permute-done((bf16[128,1536]{1,0:T(8,128)(2,1)S(1)}, bf16[128,1536]{1,0:T(8,128)(2,1)S(1)}, u32[]{:S(2)}, u32[]{:S(2)}) %collective-permute-start.13) | collective-permute-done | bytes 393248 | tf_op jit(solution)/shard_map/ppermute | solution.py:890
  59.0 5.2 %attn_fwd.5 = (bf16[1024,256]{1,0:T(8,128)(2,1)S(1)}, bf16[1024,256]{1,0:T(8,128)(2,1)S(1)}, bf16[1024,256]{1,0:T(8,128)(2,1)S(1)}, bf16[1024,256]{1,0:T(8,128)(2,1)S(1)}, bf16[1024,256]{1,0:T(8,128)(2,1)S(1)}) custom-call(s32[4]{0:T(128)S(1)} %pad_add_fusion.meta, bf16[1024,1024]{1,0:T(8,128)(2,1)S(1)} %get-tuple-element.94.source.refs_6_, ...), custom_call_target="tpu_custom_call" | custom-call | flops 8000000000 | bytes 6000000 | tf_op jit(solution)/shard_map/attn_fwd/pallas_call | solution.py:290
  67.4 5.4 %attn_fwd.7 = (bf16[1024,256]{1,0:T(8,128)(2,1)S(1)}, bf16[1024,256]{1,0:T(8,128)(2,1)S(1)}, bf16[1024,256]{1,0:T(8,128)(2,1)S(1)}, bf16[1024,256]{1,0:T(8,128)(2,1)S(1)}, bf16[1024,256]{1,0:T(8,128)(2,1)S(1)}) custom-call(s32[4]{0:T(128)S(1)} %pad_add_fusion.meta, bf16[1024,1024]{1,0:T(8,128)(2,1)S(1)} %get-tuple-element.94.source.refs_6_, ...), custom_call_target="tpu_custom_call" | custom-call | flops 8000000000 | bytes 6000000 | tf_op jit(solution)/shard_map/attn_fwd/pallas_call | solution.py:290
  73.0 5.2 %attn_fwd.6 = (bf16[1024,256]{1,0:T(8,128)(2,1)S(1)}, bf16[1024,256]{1,0:T(8,128)(2,1)S(1)}, bf16[1024,256]{1,0:T(8,128)(2,1)S(1)}, bf16[1024,256]{1,0:T(8,128)(2,1)S(1)}, bf16[1024,256]{1,0:T(8,128)(2,1)S(1)}) custom-call(s32[4]{0:T(128)S(1)} %pad_add_fusion.meta, bf16[1024,1024]{1,0:T(8,128)(2,1)S(1)} %get-tuple-element.94.source.refs_6_, ...), custom_call_target="tpu_custom_call" | custom-call | flops 8000000000 | bytes 6000000 | tf_op jit(solution)/shard_map/attn_fwd/pallas_call | solution.py:290
  79.1 7.7 %mlp_fwd_bwd.3 = (bf16[256,1024]{1,0:T(8,128)(2,1)S(1)}, bf16[256,1024]{1,0:T(8,128)(2,1)S(1)}, bf16[512,1024]{1,0:T(8,128)(2,1)S(1)}, bf16[512,1024]{1,0:T(8,12...) custom-call(s32[4]{0:T(128)S(1)} %pad_add_fusion.meta, ...), custom_call_target="tpu_custom_call" | custom-call | flops 8000000000 | bytes 16000000 | tf_op jit(solution)/shard_map/mlp_fwd_bwd/pallas_call | solution.py:396
  88.5 7.9 %mlp_fwd_bwd.2 = (bf16[256,1024]{1,0:T(8,128)(2,1)S(1)}, bf16[256,1024]{1,0:T(8,128)(2,1)S(1)}, bf16[512,1024]{1,0:T(8,128)(2,1)S(1)}, bf16[512,1024]{1,0:T(8,12...) custom-call(s32[4]{0:T(128)S(1)} %pad_add_fusion.meta, ...), custom_call_target="tpu_custom_call" | custom-call | flops 8000000000 | bytes 16000000 | tf_op jit(solution)/shard_map/mlp_fwd_bwd/pallas_call | solution.py:396
  96.9 4.7 %collective-permute-done.27 = bf16[256,1024]{1,0:T(8,128)(2,1)S(1)} collective-permute-done((bf16[256,1024]{1,0:T(8,128)(2,1)S(1)}, bf16[256,1024]{1,0:T(8,128)(2,1)S(1)}, u32[]{:S(2)}, u32[]{:S(2)}) %collective-permute-start.27) | collective-permute-done | bytes 524320 | tf_op jit(solution)/shard_map/ppermute | solution.py:931
  104.5 17.8 %collective-permute-done.21 = bf16[256,1024]{1,0:T(8,128)(2,1)S(1)} collective-permute-done((bf16[256,1024]{1,0:T(8,128)(2,1)S(1)}, bf16[256,1024]{1,0:T(8,128)(2,1)S(1)}, u32[]{:S(2)}, u32[]{:S(2)}) %collective-permute-start.21) | collective-permute-done | bytes 524320 | tf_op jit(solution)/shard_map/ppermute | solution.py:931
  127.9 11.9 %collective-permute-done.28 = bf16[256,1024]{1,0:T(8,128)(2,1)S(1)} collective-permute-done((bf16[256,1024]{1,0:T(8,128)(2,1)S(1)}, bf16[256,1024]{1,0:T(8,128)(2,1)S(1)}, u32[]{:S(2)}, u32[]{:S(2)}) %collective-permute-start.28) | collective-permute-done | bytes 524320 | tf_op jit(solution)/shard_map/ppermute | solution.py:931
  141.2 8.5 %collective-permute-done.25 = bf16[256,1024]{1,0:T(8,128)(2,1)S(1)} collective-permute-done((bf16[256,1024]{1,0:T(8,128)(2,1)S(1)}, bf16[256,1024]{1,0:T(8,128)(2,1)S(1)}, u32[]{:S(2)}, u32[]{:S(2)}) %collective-permute-start.25) | collective-permute-done | bytes 524320 | tf_op jit(solution)/shard_map/ppermute | solution.py:931
  150.7 5.9 %mlp_grads.1 = (bf16[4,128,2048]{2,1,0:T(8,128)(2,1)S(1)}, bf16[4,128,2048]{2,1,0:T(8,128)(2,1)S(1)}, f32[1,1024]{1,0:T(1,128)S(1)}, f32[1,1024]{1,0:T(1,128)S(1)}) custom-call(s32[4]{0:T(128)S(1)} %pad_add_fusion.meta, bf16[512,1024]{1,0:T(8,128)(2,1)S(1)} %get-tuple-element.100.refs_0_, bf16[512,1024]{1,0:T(8,128)(2,1)S(1)} %get-tuple-element.101.refs_1_, ...), custom_call_target="tpu_custom_call" | custom-call | flops 8000000000 | bytes 16000000 | tf_op jit(solution)/shard_map/mlp_grads/pallas_call | solution.py:508
  156.7 8.0 %collective-permute-done.22 = bf16[512,1024]{1,0:T(8,128)(2,1)S(1)} collective-permute-done((bf16[512,1024]{1,0:T(8,128)(2,1)S(1)}, bf16[512,1024]{1,0:T(8,128)(2,1)S(1)}, u32[]{:S(2)}, u32[]{:S(2)}) %collective-permute-start.22) | collective-permute-done | bytes 1048608 | tf_op jit(solution)/shard_map/ppermute | solution.py:931
  167.9 23.9 %collective-permute-done.29.refs_3_ = bf16[256,1024]{1,0:T(8,128)(2,1)S(1)} collective-permute-done((bf16[256,1024]{1,0:T(8,128)(2,1)S(1)}, bf16[256,1024]{1,0:T(8,128)(2,1)S(1)}, u32[]{:S(2)}, u32[]{:S(2)}) %collective-permute-start.29) | collective-permute-done | bytes 524320 | tf_op jit(solution)/shard_map/ppermute | solution.py:931
  191.7 9.9 %collective-permute-done.26.refs_1_ = bf16[256,1024]{1,0:T(8,128)(2,1)S(1)} collective-permute-done((bf16[256,1024]{1,0:T(8,128)(2,1)S(1)}, bf16[256,1024]{1,0:T(8,128)(2,1)S(1)}, u32[]{:S(2)}, u32[]{:S(2)}) %collective-permute-start.26) | collective-permute-done | bytes 524320 | tf_op jit(solution)/shard_map/ppermute | solution.py:931
  201.7 4.4 %norm_bwd.1 = (f32[1024,1024]{1,0:T(8,128)S(1)}, bf16[1024,1024]{1,0:T(8,128)(2,1)S(1)}, f32[1,1024]{1,0:T(1,128)S(1)}) custom-call(s32[4]{0:T(128)S(1)} %pad_add_fusion.meta, bf16[256,1024]{1,0:T(8,128)(2,1)S(1)} %add_convert_fusion.5.refs_0_, bf16[256,1024]{1,0:T(8,128)(2,1)S(1)} %collective-permute-done.26.refs_1_, ...), custom_call_target="tpu_custom_call" | custom-call | flops 1000000000 | bytes 16000000 | tf_op jit(solution)/shard_map/norm_bwd/pallas_call | solution.py:570
  206.3 14.2 %attn_bwd.4 = (f32[1024,1024]{1,0:T(8,128)S(1)}, bf16[4,128,1024]{2,1,0:T(8,128)(2,1)S(1)}, bf16[4,128,1024]{2,1,0:T(8,128)(2,1)S(1)}) custom-call(s32[4]{0:T(128)S(1)} %pad_add_fusion.meta, bf16[1024,1024]{1,0:T(8,128)(2,1)S(1)} %get-tuple-element.133.refs_0_, bf16[1024,256]{1,0:T(8,128)(2,1)S(1)} %copy-done.77, ...), custom_call_target="tpu_custom_call" | custom-call | flops 10000000000 | bytes 7000000 | tf_op jit(solution)/shard_map/attn_bwd/pallas_call | solution.py:821
  228.0 11.3 %attn_bwd.5.refs_6_ = f32[1024,1024]{1,0:T(8,128)S(1)} custom-call(s32[4]{0:T(128)S(1)} %pad_add_fusion.meta, bf16[1024,1024]{1,0:T(8,128)(2,1)S(1)} %get-tuple-element.133.refs_0_, bf16[1024,256]{1,0:T(8,128)(2,1)S(1)} %copy-done.54, bf16[1024,256]{1,0:T(8,128)(2,1)S(1)} %copy-done.56, bf16[1024,256]{1,0:T(8,128)(2,1)S(1)} %copy-done.58, ...), custom_call_target="tpu_custom_call" | custom-call | flops 10000000000 | bytes 7000000 | tf_op jit(solution)/shard_map/attn_bwd/pallas_call | solution.py:821
  247.9 11.2 %attn_bwd.6.refs_6_ = f32[1024,1024]{1,0:T(8,128)S(1)} custom-call(s32[4]{0:T(128)S(1)} %pad_add_fusion.meta, bf16[1024,1024]{1,0:T(8,128)(2,1)S(1)} %get-tuple-element.133.refs_0_, bf16[1024,256]{1,0:T(8,128)(2,1)S(1)} %copy-done.64, bf16[1024,256]{1,0:T(8,128)(2,1)S(1)} %copy-done.66, bf16[1024,256]{1,0:T(8,128)(2,1)S(1)} %copy-done.68, ...), custom_call_target="tpu_custom_call" | custom-call | flops 10000000000 | bytes 7000000 | tf_op jit(solution)/shard_map/attn_bwd/pallas_call | solution.py:821
  261.0 13.8 %attn_bwd.7 = (f32[1024,1024]{1,0:T(8,128)}, f32[4,4,128]{2,1,0:T(4,128)S(1)}, f32[4,4,128]{2,1,0:T(4,128)S(1)}) custom-call(s32[4]{0:T(128)S(1)} %pad_add_fusion.meta, bf16[1024,1024]{1,0:T(8,128)(2,1)S(1)} %get-tuple-element.133.refs_0_, bf16[1024,256]{1,0:T(8,128)(2,1)S(1)} %copy-done.44, bf16[1024,256]{1,0:T(8,128)(2,1)S(1)} %copy-done.46, ...), custom_call_target="tpu_custom_call" | custom-call | flops 10000000000 | bytes 7000000 | tf_op jit(solution)/shard_map/attn_bwd/pallas_call | solution.py:821
  286.6 5.4 %collective-permute-done.39 = f32[4,128]{1,0:T(4,128)S(1)} collective-permute-done((f32[4,128]{1,0:T(4,128)S(1)}, f32[4,128]{1,0:T(4,128)S(1)}, u32[]{:S(2)}, u32[]{:S(2)}) %collective-permute-start.39) | collective-permute-done | bytes 2080 | tf_op jit(solution)/shard_map/ppermute | solution.py:890
  (269 shorter events, 77.1 us)
Async XLA Ops:
  9.0 16.2 %collective-permute-start.4 = (bf16[144,1536]{1,0:T(8,128)(2,1)S(1)}, bf16[144,1536]{1,0:T(8,128)(2,1)S(1)}, u32[]{:S(2)}, u32[]{:S(2)}) collective-permute-start(bf16[144,1536]{1,0:T(8,128)(2,1)S(1)} %prep_first.1.refs_0_.refs_19_.refs_15_), channel_id=1, source_target_pairs={{0,16},{4,12},{8,24},{12,4},{16,0},{20,28},{24,8},{28,20},{1,17},{... | collective-permute-start | bytes 1327112 | tf_op jit(solution)/shard_map/ppermute | solution.py:890
  21.8 19.4 %collective-permute-start.8 = (bf16[128,3072]{1,0:T(8,128)(2,1)S(1)}, bf16[128,3072]{1,0:T(8,128)(2,1)S(1)}, u32[]{:S(2)}, u32[]{:S(2)}) collective-permute-start(bf16[128,3072]{1,0:T(8,128)(2,1)S(1)} %get-tuple-element.93.refs_8_.refs_2_.refs_11_.refs_7_.refs_13_), channel_id=1, source_target_pairs={{0,8},{4,20},{8,0},{12,28},{16,24},{20,4},{24,16},{28,12},{1,9},{5... | collective-permute-start | bytes 2359304 | tf_op jit(solution)/shard_map/ppermute | solution.py:890
  39.8 26.8 %collective-permute-start.17 = (bf16[128,3072]{1,0:T(8,128)(2,1)S(1)}, bf16[128,3072]{1,0:T(8,128)(2,1)S(1)}, u32[]{:S(2)}, u32[]{:S(2)}) collective-permute-start(bf16[128,3072]{1,0:T(8,128)(2,1)S(1)} %get-tuple-element.93.refs_8_.refs_2_.refs_11_.refs_7_.refs_13_), channel_id=1, source_target_pairs={{0,16},{4,12},{8,24},{12,4},{16,0},{20,28},{24,8},{28,20},{1,17},{... | collective-permute-start | bytes 2359304 | tf_op jit(solution)/shard_map/ppermute | solution.py:890
  41.3 17.7 %collective-permute-start.13 = (bf16[128,1536]{1,0:T(8,128)(2,1)S(1)}, bf16[128,1536]{1,0:T(8,128)(2,1)S(1)}, u32[]{:S(2)}, u32[]{:S(2)}) collective-permute-start(bf16[128,1536]{1,0:T(8,128)(2,1)S(1)} %collective-permute-done.1.refs_2_.refs_17_.refs_23_), channel_id=1, source_target_pairs={{0,16},{4,12},{8,24},{12,4},{16,0},{20,28},{24,8},{28,20},{1,17},{... | collective-permute-start | bytes 1179656 | tf_op jit(solution)/shard_map/ppermute | solution.py:890
  41.8 25.6 %collective-permute-start.19 = (bf16[128,3072]{1,0:T(8,128)(2,1)S(1)}, bf16[128,3072]{1,0:T(8,128)(2,1)S(1)}, u32[]{:S(2)}, u32[]{:S(2)}) collective-permute-start(bf16[128,3072]{1,0:T(8,128)(2,1)S(1)} %collective-permute-done.8.refs_10_.refs_4_.refs_13_.refs_9_.refs_15_), channel_id=1, source_target_pairs={{0,16},{4,12},{8,24},{12,4},{16,0},{20,28},{24,8},{28,20},{1,17},{... | collective-permute-start | bytes 2359304 | tf_op jit(solution)/shard_map/ppermute | solution.py:890
  51.8 14.6 %collective-permute-start.12 = (bf16[128,1536]{1,0:T(8,128)(2,1)S(1)}, bf16[128,1536]{1,0:T(8,128)(2,1)S(1)}, u32[]{:S(2)}, u32[]{:S(2)}) collective-permute-start(bf16[128,1536]{1,0:T(8,128)(2,1)S(1)} %collective-permute-done.11.refs_4_.refs_19_.refs_25_), channel_id=1, source_target_pairs={{0,4},{4,0},{8,12},{12,8},{16,20},{20,16},{24,28},{28,24},{1,5},{5... | collective-permute-start | bytes 1179656 | tf_op jit(solution)/shard_map/ppermute | solution.py:890
  86.8 14.8 %collective-permute-start.27 = (bf16[256,1024]{1,0:T(8,128)(2,1)S(1)}, bf16[256,1024]{1,0:T(8,128)(2,1)S(1)}, u32[]{:S(2)}, u32[]{:S(2)}) collective-permute-start(bf16[256,1024]{1,0:T(8,128)(2,1)S(1)} %get-tuple-element.108), channel_id=1, source_target_pairs={{0,1},{1,0},{2,3},{3,2},{4,5},{5,4},{6,7},{7,6},{8,9},{9,8},{10,11... | collective-permute-start | bytes 1572872 | tf_op jit(solution)/shard_map/ppermute | solution.py:931
  96.4 25.9 %collective-permute-start.21 = (bf16[256,1024]{1,0:T(8,128)(2,1)S(1)}, bf16[256,1024]{1,0:T(8,128)(2,1)S(1)}, u32[]{:S(2)}, u32[]{:S(2)}) collective-permute-start(bf16[256,1024]{1,0:T(8,128)(2,1)S(1)} %get-tuple-element.105), channel_id=1, source_target_pairs={{0,1},{1,0},{2,3},{3,2},{4,5},{5,4},{6,7},{7,6},{8,9},{9,8},{10,11... | collective-permute-start | bytes 1572872 | tf_op jit(solution)/shard_map/ppermute | solution.py:931
  101.8 37.9 %collective-permute-start.28 = (bf16[256,1024]{1,0:T(8,128)(2,1)S(1)}, bf16[256,1024]{1,0:T(8,128)(2,1)S(1)}, u32[]{:S(2)}, u32[]{:S(2)}) collective-permute-start(bf16[256,1024]{1,0:T(8,128)(2,1)S(1)} %add_convert_fusion.4), channel_id=1, source_target_pairs={{0,2},{1,3},{2,0},{3,1},{4,6},{5,7},{6,4},{7,5},{8,10},{9,11},{10,... | collective-permute-start | bytes 1572872 | tf_op jit(solution)/shard_map/ppermute | solution.py:931
  122.5 27.2 %collective-permute-start.25 = (bf16[256,1024]{1,0:T(8,128)(2,1)S(1)}, bf16[256,1024]{1,0:T(8,128)(2,1)S(1)}, u32[]{:S(2)}, u32[]{:S(2)}) collective-permute-start(bf16[256,1024]{1,0:T(8,128)(2,1)S(1)} %add_convert_fusion.6), channel_id=1, source_target_pairs={{0,2},{1,3},{2,0},{3,1},{4,6},{5,7},{6,4},{7,5},{8,10},{9,11},{10,... | collective-permute-start | bytes 1572872 | tf_op jit(solution)/shard_map/ppermute | solution.py:931
  126.0 38.7 %collective-permute-start.22 = (bf16[512,1024]{1,0:T(8,128)(2,1)S(1)}, bf16[512,1024]{1,0:T(8,128)(2,1)S(1)}, u32[]{:S(2)}, u32[]{:S(2)}) collective-permute-start(bf16[512,1024]{1,0:T(8,128)(2,1)S(1)} %get-tuple-element.106), channel_id=1, source_target_pairs={{0,1},{1,0},{2,3},{3,2},{4,5},{5,4},{6,7},{7,6},{8,9},{9,8},{10,11... | collective-permute-start | bytes 3145736 | tf_op jit(solution)/shard_map/ppermute | solution.py:931
  140.0 51.8 %collective-permute-start.29 = (bf16[256,1024]{1,0:T(8,128)(2,1)S(1)}, bf16[256,1024]{1,0:T(8,128)(2,1)S(1)}, u32[]{:S(2)}, u32[]{:S(2)}) collective-permute-start(bf16[256,1024]{1,0:T(8,128)(2,1)S(1)} %add_convert_fusion.3.refs_2_), channel_id=1, source_target_pairs={{0,1},{1,0},{2,3},{3,2},{4,5},{5,4},{6,7},{7,6},{8,9},{9,8},{10,11... | collective-permute-start | bytes 1572872 | tf_op jit(solution)/shard_map/ppermute | solution.py:931
  149.9 51.7 %collective-permute-start.26 = (bf16[256,1024]{1,0:T(8,128)(2,1)S(1)}, bf16[256,1024]{1,0:T(8,128)(2,1)S(1)}, u32[]{:S(2)}, u32[]{:S(2)}) collective-permute-start(bf16[256,1024]{1,0:T(8,128)(2,1)S(1)} %add_convert_fusion.5.refs_0_), channel_id=1, source_target_pairs={{0,1},{1,0},{2,3},{3,2},{4,5},{5,4},{6,7},{7,6},{8,9},{9,8},{10,11... | collective-permute-start | bytes 1572872 | tf_op jit(solution)/shard_map/ppermute | solution.py:931
  156.6 64.4 %collective-permute-start.41 = (bf16[4,128,2048]{2,1,0:T(8,128)(2,1)S(1)}, bf16[4,128,2048]{2,1,0:T(8,128)(2,1)}, u32[]{:S(2)}, u32[]{:S(2)}) collective-permute-start(bf16[4,128,2048]{2,1,0:T(8,128)(2,1)S(1)} %get-tuple-element.153), channel_id=1, source_target_pairs={{0,4},{4,0},{8,12},{12,8},{16,20},{20,16},{24,28},{28,24},{1,5},{5... | collective-permute-start | bytes 6291464 | tf_op jit(solution)/shard_map/ppermute | solution.py:890
  165.1 55.4 %collective-permute-start.23 = (bf16[512,1024]{1,0:T(8,128)(2,1)S(1)}, bf16[512,1024]{1,0:T(8,128)(2,1)S(1)}, u32[]{:S(2)}, u32[]{:S(2)}) collective-permute-start(bf16[512,1024]{1,0:T(8,128)(2,1)S(1)} %add_convert_fusion.2), channel_id=1, source_target_pairs={{0,2},{1,3},{2,0},{3,1},{4,6},{5,7},{6,4},{7,5},{8,10},{9,11},{10,... | collective-permute-start | bytes 3145736 | tf_op jit(solution)/shard_map/ppermute | solution.py:931
  223.6 51.3 %collective-permute-start.24 = (bf16[512,1024]{1,0:T(8,128)(2,1)S(1)}, bf16[512,1024]{1,0:T(8,128)(2,1)S(1)}, u32[]{:S(2)}, u32[]{:S(2)}) collective-permute-start(bf16[512,1024]{1,0:T(8,128)(2,1)S(1)} %add_convert_fusion.1.refs_2_), channel_id=1, source_target_pairs={{0,1},{1,0},{2,3},{3,2},{4,5},{5,4},{6,7},{7,6},{8,9},{9,8},{10,11... | collective-permute-start | bytes 3145736 | tf_op jit(solution)/shard_map/ppermute | solution.py:931
  224.2 17.1 %collective-permute-start.31 = (bf16[128,1024]{1,0:T(8,128)(2,1)S(1)}, bf16[128,1024]{1,0:T(8,128)(2,1)S(1)}, u32[]{:S(2)}, u32[]{:S(2)}) collective-permute-start(bf16[128,1024]{1,0:T(8,128)(2,1)S(1)} %get-tuple-element.170), channel_id=1, source_target_pairs={{0,8},{4,12},{8,0},{12,4},{16,24},{20,28},{24,16},{28,20},{1,9},{5... | collective-permute-start | bytes 786440 | tf_op jit(solution)/shard_map/ppermute | solution.py:890
  226.2 15.1 %collective-permute-start.32 = (bf16[128,1024]{1,0:T(8,128)(2,1)S(1)}, bf16[128,1024]{1,0:T(8,128)(2,1)S(1)}, u32[]{:S(2)}, u32[]{:S(2)}) collective-permute-start(bf16[128,1024]{1,0:T(8,128)(2,1)S(1)} %get-tuple-element.172), channel_id=1, source_target_pairs={{0,16},{4,20},{8,24},{12,28},{16,0},{20,4},{24,8},{28,12},{1,17},{... | collective-permute-start | bytes 786440 | tf_op jit(solution)/shard_map/ppermute | solution.py:890
  226.7 14.6 %collective-permute-start.33 = (bf16[128,1024]{1,0:T(8,128)(2,1)S(1)}, bf16[128,1024]{1,0:T(8,128)(2,1)S(1)}, u32[]{:S(2)}, u32[]{:S(2)}) collective-permute-start(bf16[128,1024]{1,0:T(8,128)(2,1)S(1)} %get-tuple-element.171), channel_id=1, source_target_pairs={{0,24},{4,28},{8,16},{12,20},{16,8},{20,12},{24,0},{28,4},{1,25},{... | collective-permute-start | bytes 786440 | tf_op jit(solution)/shard_map/ppermute | solution.py:890
  241.5 17.6 %collective-permute-start.34 = (bf16[128,1024]{1,0:T(8,128)(2,1)S(1)}, bf16[128,1024]{1,0:T(8,128)(2,1)S(1)}, u32[]{:S(2)}, u32[]{:S(2)}) collective-permute-start(bf16[128,1024]{1,0:T(8,128)(2,1)S(1)} %fusion.8.refs_0_), channel_id=1, source_target_pairs={{0,2},{1,3},{2,0},{3,1},{4,6},{5,7},{6,4},{7,5},{8,10},{9,11},{10,... | collective-permute-start | bytes 786440 | tf_op jit(solution)/shard_map/ppermute | solution.py:931
  243.5 31.4 %collective-permute-start.35 = (bf16[128,1024]{1,0:T(8,128)(2,1)S(1)}, bf16[128,1024]{1,0:T(8,128)(2,1)S(1)}, u32[]{:S(2)}, u32[]{:S(2)}) collective-permute-start(bf16[128,1024]{1,0:T(8,128)(2,1)S(1)} %fusion.8.refs_0_), channel_id=1, source_target_pairs={{0,1},{1,0},{2,3},{3,2},{4,5},{5,4},{6,7},{7,6},{8,9},{9,8},{10,11... | collective-permute-start | bytes 786440 | tf_op jit(solution)/shard_map/ppermute | solution.py:931
  243.6 32.5 %collective-permute-start.42 = (bf16[2,128,2048]{2,1,0:T(8,128)(2,1)S(1)}, bf16[2,128,2048]{2,1,0:T(8,128)(2,1)S(1)}, u32[]{:S(2)}, u32[]{:S(2)}) collective-permute-start(bf16[2,128,2048]{2,1,0:T(8,128)(2,1)S(1)} %copy-done.80), channel_id=1, source_target_pairs={{0,8},{4,12},{8,0},{12,4},{16,24},{20,28},{24,16},{28,20},{1,9},{5... | collective-permute-start | bytes 3145736 | tf_op jit(solution)/shard_map/ppermute | solution.py:890
  259.0 15.8 %collective-permute-start.36 = (bf16[128,1024]{1,0:T(8,128)(2,1)S(1)}, bf16[128,1024]{1,0:T(8,128)(2,1)S(1)}, u32[]{:S(2)}, u32[]{:S(2)}) collective-permute-start(bf16[128,1024]{1,0:T(8,128)(2,1)S(1)} %collective-permute-done.34.refs_2_), channel_id=1, source_target_pairs={{0,1},{1,0},{2,3},{3,2},{4,5},{5,4},{6,7},{7,6},{8,9},{9,8},{10,11... | collective-permute-start | bytes 786440 | tf_op jit(solution)/shard_map/ppermute | solution.py:931
  277.9 14.7 %collective-permute-start.43 = (bf16[128,2048]{1,0:T(8,128)(2,1)S(1)}, bf16[128,2048]{1,0:T(8,128)(2,1)S(1)}, u32[]{:S(2)}, u32[]{:S(2)}) collective-permute-start(bf16[128,2048]{1,0:T(8,128)(2,1)S(1)} %fusion.4), channel_id=1, source_target_pairs={{0,16},{4,20},{8,24},{12,28},{16,0},{20,4},{24,8},{28,12},{1,17},{... | collective-permute-start | bytes 1572872 | tf_op jit(solution)/shard_map/ppermute | solution.py:890
  (101 other events, 1482.9 us)

commit v2 on v1

--- a/solution.py
+++ b/solution.py
@@ -977,7 +977,7 @@
         second, third = prep_rest(meta, groups, per, *raw)
         bundles.append(gather_pieces(second))
         rest = gather_pieces(after(third, bundles[0][2]))
-        heads = [attn_fwd(meta, after(normed_one, bundles[1][2]), bundles[0], groups, 0, 4)]
+        heads = [attn_fwd(meta, normed_one, bundles[0], groups, 0, 4)]
         attn_in, vec = heads[0][5:]
         bias = vec[2:3]
         heads.append(attn_fwd(meta, attn_in, bundles[0], groups, 1, 0))

time: 298 us -> 298 us (level)
  no operation moved by 1% of the time
where the time goes in v2:
time: 298 us; the launch traced here: 295 us
  waiting for transfers between devices  118 us (40%)
  Pallas kernels  108 us (36%)
  starting transfers between devices  41.2 us (14%)
  local copies, waits for them, and re-layouts  15.1 us (5%)
  other arithmetic  9.84 us (3%)
    ppermute x12, waiting for transfers between devices, swapped(): return lax.ppermute(arr, 'mp', [(i, i ^ bits) for i in range(4)])  84.7 us
    pallas_call x4, Pallas kernels, attn_bwd(): pl.pallas_call(functools.partial(attn_bwd_kernel, shape), grid=(count,),...  50.5 us
    ppermute x32, waiting for transfers between devices, send(): return lax.ppermute(arr, 'dp', [(i, move(i)) for i in range(PAIRED)])  33.1 us
    ppermute x32, starting transfers between devices, send(): return lax.ppermute(arr, 'dp', [(i, move(i)) for i in range(PAIRED)])  25.5 us
    pallas_call x4, Pallas kernels, attn_fwd(): pl.pallas_call(functools.partial(attn_fwd_kernel, n, count_vec, position...  22.5 us
    ppermute x12, starting transfers between devices, swapped(): return lax.ppermute(arr, 'mp', [(i, i ^ bits) for i in range(4)])  15.7 us
    pallas_call x2, Pallas kernels, mlp(): pl.pallas_call(functools.partial(mlp_kernel, n, n_atts, groups, part), ou...  15.6 us
    unnamed x163, local copies, waits for them, and re-layouts  13.5 us
  transfers between devices with their start and end apart: 44, of which 14 were waited for; matrix products, arithmetic and copies ran while one was open for 3% of the time, Pallas kernels for 34%

profile of v2, /device:TPU:0, one launch (start us, length us, event | category | flops | bytes accessed | tf_op | source)
XLA Modules:
  0.0 294.8 jit_solution(9905927386868079898)
XLA Ops:
  12.5 7.0 %collective-permute-done.1.refs_2_.refs_21_.refs_17_ = bf16[144,1536]{1,0:T(8,128)(2,1)S(1)} collective-permute-done((bf16[144,1536]{1,0:T(8,128)(2,1)S(1)}, bf16[144,1536]{1,0:T(8,128)(2,1)S(1)}, u32[]{:S(2)}, u32[]{:S(2)}) %collective-permute-start.1) | collective-permute-done | bytes 442400 | tf_op jit(solution)/shard_map/ppermute | solution.py:890
  25.7 6.8 %collective-permute-done.5.refs_6_.refs_25_.refs_21_ = bf16[144,1536]{1,0:T(8,128)(2,1)S(1)} collective-permute-done((bf16[144,1536]{1,0:T(8,128)(2,1)S(1)}, bf16[144,1536]{1,0:T(8,128)(2,1)S(1)}, u32[]{:S(2)}, u32[]{:S(2)}) %collective-permute-start.5) | collective-permute-done | bytes 442400 | tf_op jit(solution)/shard_map/ppermute | solution.py:890
  33.0 5.5 %collective-permute-done.9.refs_2_.refs_17_.refs_23_ = bf16[128,1536]{1,0:T(8,128)(2,1)S(1)} collective-permute-done((bf16[128,1536]{1,0:T(8,128)(2,1)S(1)}, bf16[128,1536]{1,0:T(8,128)(2,1)S(1)}, u32[]{:S(2)}, u32[]{:S(2)}) %collective-permute-start.9) | collective-permute-done | bytes 393248 | tf_op jit(solution)/shard_map/ppermute | solution.py:890
  43.3 6.7 %attn_fwd.4 = (bf16[1024,256]{1,0:T(8,128)(2,1)S(1)}, bf16[1024,256]{1,0:T(8,128)(2,1)S(1)}, bf16[1024,256]{1,0:T(8,128)(2,1)S(1)}, bf16[1024,256]{1,0:T(8,128)(...) custom-call(s32[4]{0:T(128)S(1)} %pad_add_fusion.meta, ...), custom_call_target="tpu_custom_call" | custom-call | flops 8000000000 | bytes 6000000 | tf_op jit(solution)/shard_map/attn_fwd/pallas_call | solution.py:290
  52.3 6.7 %collective-permute-done.13.refs_6_.refs_21_.refs_27_ = bf16[128,1536]{1,0:T(8,128)(2,1)S(1)} collective-permute-done((bf16[128,1536]{1,0:T(8,128)(2,1)S(1)}, bf16[128,1536]{1,0:T(8,128)(2,1)S(1)}, u32[]{:S(2)}, u32[]{:S(2)}) %collective-permute-start.13) | collective-permute-done | bytes 393248 | tf_op jit(solution)/shard_map/ppermute | solution.py:890
  59.0 5.2 %attn_fwd.5 = (bf16[1024,256]{1,0:T(8,128)(2,1)S(1)}, bf16[1024,256]{1,0:T(8,128)(2,1)S(1)}, bf16[1024,256]{1,0:T(8,128)(2,1)S(1)}, bf16[1024,256]{1,0:T(8,128)(2,1)S(1)}, bf16[1024,256]{1,0:T(8,128)(2,1)S(1)}) custom-call(s32[4]{0:T(128)S(1)} %pad_add_fusion.meta, bf16[1024,1024]{1,0:T(8,128)(2,1)S(1)} %get-tuple-element.91.source.refs_6_, ...), custom_call_target="tpu_custom_call" | custom-call | flops 8000000000 | bytes 6000000 | tf_op jit(solution)/shard_map/attn_fwd/pallas_call | solution.py:290
  67.4 5.4 %attn_fwd.7 = (bf16[1024,256]{1,0:T(8,128)(2,1)S(1)}, bf16[1024,256]{1,0:T(8,128)(2,1)S(1)}, bf16[1024,256]{1,0:T(8,128)(2,1)S(1)}, bf16[1024,256]{1,0:T(8,128)(2,1)S(1)}, bf16[1024,256]{1,0:T(8,128)(2,1)S(1)}) custom-call(s32[4]{0:T(128)S(1)} %pad_add_fusion.meta, bf16[1024,1024]{1,0:T(8,128)(2,1)S(1)} %get-tuple-element.91.source.refs_6_, ...), custom_call_target="tpu_custom_call" | custom-call | flops 8000000000 | bytes 6000000 | tf_op jit(solution)/shard_map/attn_fwd/pallas_call | solution.py:290
  73.0 5.2 %attn_fwd.6 = (bf16[1024,256]{1,0:T(8,128)(2,1)S(1)}, bf16[1024,256]{1,0:T(8,128)(2,1)S(1)}, bf16[1024,256]{1,0:T(8,128)(2,1)S(1)}, bf16[1024,256]{1,0:T(8,128)(2,1)S(1)}, bf16[1024,256]{1,0:T(8,128)(2,1)S(1)}) custom-call(s32[4]{0:T(128)S(1)} %pad_add_fusion.meta, bf16[1024,1024]{1,0:T(8,128)(2,1)S(1)} %get-tuple-element.91.source.refs_6_, ...), custom_call_target="tpu_custom_call" | custom-call | flops 8000000000 | bytes 6000000 | tf_op jit(solution)/shard_map/attn_fwd/pallas_call | solution.py:290
  79.1 7.7 %mlp_fwd_bwd.3 = (bf16[256,1024]{1,0:T(8,128)(2,1)S(1)}, bf16[256,1024]{1,0:T(8,128)(2,1)S(1)}, bf16[512,1024]{1,0:T(8,128)(2,1)S(1)}, bf16[512,1024]{1,0:T(8,12...) custom-call(s32[4]{0:T(128)S(1)} %pad_add_fusion.meta, ...), custom_call_target="tpu_custom_call" | custom-call | flops 8000000000 | bytes 16000000 | tf_op jit(solution)/shard_map/mlp_fwd_bwd/pallas_call | solution.py:396
  88.5 7.9 %mlp_fwd_bwd.2 = (bf16[256,1024]{1,0:T(8,128)(2,1)S(1)}, bf16[256,1024]{1,0:T(8,128)(2,1)S(1)}, bf16[512,1024]{1,0:T(8,128)(2,1)S(1)}, bf16[512,1024]{1,0:T(8,12...) custom-call(s32[4]{0:T(128)S(1)} %pad_add_fusion.meta, ...), custom_call_target="tpu_custom_call" | custom-call | flops 8000000000 | bytes 16000000 | tf_op jit(solution)/shard_map/mlp_fwd_bwd/pallas_call | solution.py:396
  96.9 4.7 %collective-permute-done.27 = bf16[256,1024]{1,0:T(8,128)(2,1)S(1)} collective-permute-done((bf16[256,1024]{1,0:T(8,128)(2,1)S(1)}, bf16[256,1024]{1,0:T(8,128)(2,1)S(1)}, u32[]{:S(2)}, u32[]{:S(2)}) %collective-permute-start.27) | collective-permute-done | bytes 524320 | tf_op jit(solution)/shard_map/ppermute | solution.py:931
  104.5 17.8 %collective-permute-done.21 = bf16[256,1024]{1,0:T(8,128)(2,1)S(1)} collective-permute-done((bf16[256,1024]{1,0:T(8,128)(2,1)S(1)}, bf16[256,1024]{1,0:T(8,128)(2,1)S(1)}, u32[]{:S(2)}, u32[]{:S(2)}) %collective-permute-start.21) | collective-permute-done | bytes 524320 | tf_op jit(solution)/shard_map/ppermute | solution.py:931
  127.9 11.9 %collective-permute-done.28 = bf16[256,1024]{1,0:T(8,128)(2,1)S(1)} collective-permute-done((bf16[256,1024]{1,0:T(8,128)(2,1)S(1)}, bf16[256,1024]{1,0:T(8,128)(2,1)S(1)}, u32[]{:S(2)}, u32[]{:S(2)}) %collective-permute-start.28) | collective-permute-done | bytes 524320 | tf_op jit(solution)/shard_map/ppermute | solution.py:931
  141.2 8.5 %collective-permute-done.25 = bf16[256,1024]{1,0:T(8,128)(2,1)S(1)} collective-permute-done((bf16[256,1024]{1,0:T(8,128)(2,1)S(1)}, bf16[256,1024]{1,0:T(8,128)(2,1)S(1)}, u32[]{:S(2)}, u32[]{:S(2)}) %collective-permute-start.25) | collective-permute-done | bytes 524320 | tf_op jit(solution)/shard_map/ppermute | solution.py:931
  150.7 5.9 %mlp_grads.1 = (bf16[4,128,2048]{2,1,0:T(8,128)(2,1)S(1)}, bf16[4,128,2048]{2,1,0:T(8,128)(2,1)S(1)}, f32[1,1024]{1,0:T(1,128)S(1)}, f32[1,1024]{1,0:T(1,128)S(1)}) custom-call(s32[4]{0:T(128)S(1)} %pad_add_fusion.meta, bf16[512,1024]{1,0:T(8,128)(2,1)S(1)} %get-tuple-element.98.refs_0_, bf16[512,1024]{1,0:T(8,128)(2,1)S(1)} %get-tuple-element.99.refs_1_, ...), custom_call_target="tpu_custom_call" | custom-call | flops 8000000000 | bytes 16000000 | tf_op jit(solution)/shard_map/mlp_grads/pallas_call | solution.py:508
  156.7 8.0 %collective-permute-done.22 = bf16[512,1024]{1,0:T(8,128)(2,1)S(1)} collective-permute-done((bf16[512,1024]{1,0:T(8,128)(2,1)S(1)}, bf16[512,1024]{1,0:T(8,128)(2,1)S(1)}, u32[]{:S(2)}, u32[]{:S(2)}) %collective-permute-start.22) | collective-permute-done | bytes 1048608 | tf_op jit(solution)/shard_map/ppermute | solution.py:931
  167.9 23.9 %collective-permute-done.29.refs_3_ = bf16[256,1024]{1,0:T(8,128)(2,1)S(1)} collective-permute-done((bf16[256,1024]{1,0:T(8,128)(2,1)S(1)}, bf16[256,1024]{1,0:T(8,128)(2,1)S(1)}, u32[]{:S(2)}, u32[]{:S(2)}) %collective-permute-start.29) | collective-permute-done | bytes 524320 | tf_op jit(solution)/shard_map/ppermute | solution.py:931
  191.7 9.9 %collective-permute-done.26.refs_1_ = bf16[256,1024]{1,0:T(8,128)(2,1)S(1)} collective-permute-done((bf16[256,1024]{1,0:T(8,128)(2,1)S(1)}, bf16[256,1024]{1,0:T(8,128)(2,1)S(1)}, u32[]{:S(2)}, u32[]{:S(2)}) %collective-permute-start.26) | collective-permute-done | bytes 524320 | tf_op jit(solution)/shard_map/ppermute | solution.py:931
  201.7 4.4 %norm_bwd.1 = (f32[1024,1024]{1,0:T(8,128)S(1)}, bf16[1024,1024]{1,0:T(8,128)(2,1)S(1)}, f32[1,1024]{1,0:T(1,128)S(1)}) custom-call(s32[4]{0:T(128)S(1)} %pad_add_fusion.meta, bf16[256,1024]{1,0:T(8,128)(2,1)S(1)} %add_convert_fusion.5.refs_0_, bf16[256,1024]{1,0:T(8,128)(2,1)S(1)} %collective-permute-done.26.refs_1_, ...), custom_call_target="tpu_custom_call" | custom-call | flops 1000000000 | bytes 16000000 | tf_op jit(solution)/shard_map/norm_bwd/pallas_call | solution.py:570
  206.3 14.2 %attn_bwd.4 = (f32[1024,1024]{1,0:T(8,128)S(1)}, bf16[4,128,1024]{2,1,0:T(8,128)(2,1)S(1)}, bf16[4,128,1024]{2,1,0:T(8,128)(2,1)S(1)}) custom-call(s32[4]{0:T(128)S(1)} %pad_add_fusion.meta, bf16[1024,1024]{1,0:T(8,128)(2,1)S(1)} %get-tuple-element.131.refs_0_, bf16[1024,256]{1,0:T(8,128)(2,1)S(1)} %copy-done.77, ...), custom_call_target="tpu_custom_call" | custom-call | flops 10000000000 | bytes 7000000 | tf_op jit(solution)/shard_map/attn_bwd/pallas_call | solution.py:821
  228.0 11.3 %attn_bwd.5.refs_6_ = f32[1024,1024]{1,0:T(8,128)S(1)} custom-call(s32[4]{0:T(128)S(1)} %pad_add_fusion.meta, bf16[1024,1024]{1,0:T(8,128)(2,1)S(1)} %get-tuple-element.131.refs_0_, bf16[1024,256]{1,0:T(8,128)(2,1)S(1)} %copy-done.54, bf16[1024,256]{1,0:T(8,128)(2,1)S(1)} %copy-done.56, bf16[1024,256]{1,0:T(8,128)(2,1)S(1)} %copy-done.58, ...), custom_call_target="tpu_custom_call" | custom-call | flops 10000000000 | bytes 7000000 | tf_op jit(solution)/shard_map/attn_bwd/pallas_call | solution.py:821
  247.9 11.2 %attn_bwd.6.refs_6_ = f32[1024,1024]{1,0:T(8,128)S(1)} custom-call(s32[4]{0:T(128)S(1)} %pad_add_fusion.meta, bf16[1024,1024]{1,0:T(8,128)(2,1)S(1)} %get-tuple-element.131.refs_0_, bf16[1024,256]{1,0:T(8,128)(2,1)S(1)} %copy-done.64, bf16[1024,256]{1,0:T(8,128)(2,1)S(1)} %copy-done.66, bf16[1024,256]{1,0:T(8,128)(2,1)S(1)} %copy-done.68, ...), custom_call_target="tpu_custom_call" | custom-call | flops 10000000000 | bytes 7000000 | tf_op jit(solution)/shard_map/attn_bwd/pallas_call | solution.py:821
  261.0 13.8 %attn_bwd.7 = (f32[1024,1024]{1,0:T(8,128)}, f32[4,4,128]{2,1,0:T(4,128)S(1)}, f32[4,4,128]{2,1,0:T(4,128)S(1)}) custom-call(s32[4]{0:T(128)S(1)} %pad_add_fusion.meta, bf16[1024,1024]{1,0:T(8,128)(2,1)S(1)} %get-tuple-element.131.refs_0_, bf16[1024,256]{1,0:T(8,128)(2,1)S(1)} %copy-done.44, bf16[1024,256]{1,0:T(8,128)(2,1)S(1)} %copy-done.46, ...), custom_call_target="tpu_custom_call" | custom-call | flops 10000000000 | bytes 7000000 | tf_op jit(solution)/shard_map/attn_bwd/pallas_call | solution.py:821
  286.6 5.4 %collective-permute-done.39 = f32[4,128]{1,0:T(4,128)S(1)} collective-permute-done((f32[4,128]{1,0:T(4,128)S(1)}, f32[4,128]{1,0:T(4,128)S(1)}, u32[]{:S(2)}, u32[]{:S(2)}) %collective-permute-start.39) | collective-permute-done | bytes 2080 | tf_op jit(solution)/shard_map/ppermute | solution.py:890
  (269 shorter events, 77.1 us)
Async XLA Ops:
  9.0 16.2 %collective-permute-start.3 = (bf16[144,1536]{1,0:T(8,128)(2,1)S(1)}, bf16[144,1536]{1,0:T(8,128)(2,1)S(1)}, u32[]{:S(2)}, u32[]{:S(2)}) collective-permute-start(bf16[144,1536]{1,0:T(8,128)(2,1)S(1)} %prep_first.1.refs_0_.refs_19_.refs_15_), channel_id=1, source_target_pairs={{0,16},{4,12},{8,24},{12,4},{16,0},{20,28},{24,8},{28,20},{1,17},{... | collective-permute-start | bytes 1327112 | tf_op jit(solution)/shard_map/ppermute | solution.py:890
  21.8 19.4 %collective-permute-start.7 = (bf16[128,3072]{1,0:T(8,128)(2,1)S(1)}, bf16[128,3072]{1,0:T(8,128)(2,1)S(1)}, u32[]{:S(2)}, u32[]{:S(2)}) collective-permute-start(bf16[128,3072]{1,0:T(8,128)(2,1)S(1)} %get-tuple-element.90.refs_8_.refs_2_.refs_11_.refs_7_.refs_13_), channel_id=1, source_target_pairs={{0,8},{4,20},{8,0},{12,28},{16,24},{20,4},{24,16},{28,12},{1,9},{5... | collective-permute-start | bytes 2359304 | tf_op jit(solution)/shard_map/ppermute | solution.py:890
  39.8 26.8 %collective-permute-start.17 = (bf16[128,3072]{1,0:T(8,128)(2,1)S(1)}, bf16[128,3072]{1,0:T(8,128)(2,1)S(1)}, u32[]{:S(2)}, u32[]{:S(2)}) collective-permute-start(bf16[128,3072]{1,0:T(8,128)(2,1)S(1)} %get-tuple-element.90.refs_8_.refs_2_.refs_11_.refs_7_.refs_13_), channel_id=1, source_target_pairs={{0,16},{4,12},{8,24},{12,4},{16,0},{20,28},{24,8},{28,20},{1,17},{... | collective-permute-start | bytes 2359304 | tf_op jit(solution)/shard_map/ppermute | solution.py:890
  41.3 17.7 %collective-permute-start.13 = (bf16[128,1536]{1,0:T(8,128)(2,1)S(1)}, bf16[128,1536]{1,0:T(8,128)(2,1)S(1)}, u32[]{:S(2)}, u32[]{:S(2)}) collective-permute-start(bf16[128,1536]{1,0:T(8,128)(2,1)S(1)} %collective-permute-done.9.refs_2_.refs_17_.refs_23_), channel_id=1, source_target_pairs={{0,16},{4,12},{8,24},{12,4},{16,0},{20,28},{24,8},{28,20},{1,17},{... | collective-permute-start | bytes 1179656 | tf_op jit(solution)/shard_map/ppermute | solution.py:890
  41.8 25.6 %collective-permute-start.19 = (bf16[128,3072]{1,0:T(8,128)(2,1)S(1)}, bf16[128,3072]{1,0:T(8,128)(2,1)S(1)}, u32[]{:S(2)}, u32[]{:S(2)}) collective-permute-start(bf16[128,3072]{1,0:T(8,128)(2,1)S(1)} %collective-permute-done.7.refs_10_.refs_4_.refs_13_.refs_9_.refs_15_), channel_id=1, source_target_pairs={{0,16},{4,12},{8,24},{12,4},{16,0},{20,28},{24,8},{28,20},{1,17},{... | collective-permute-start | bytes 2359304 | tf_op jit(solution)/shard_map/ppermute | solution.py:890
  51.8 14.6 %collective-permute-start.12 = (bf16[128,1536]{1,0:T(8,128)(2,1)S(1)}, bf16[128,1536]{1,0:T(8,128)(2,1)S(1)}, u32[]{:S(2)}, u32[]{:S(2)}) collective-permute-start(bf16[128,1536]{1,0:T(8,128)(2,1)S(1)} %collective-permute-done.11.refs_4_.refs_19_.refs_25_), channel_id=1, source_target_pairs={{0,4},{4,0},{8,12},{12,8},{16,20},{20,16},{24,28},{28,24},{1,5},{5... | collective-permute-start | bytes 1179656 | tf_op jit(solution)/shard_map/ppermute | solution.py:890
  86.8 14.8 %collective-permute-start.27 = (bf16[256,1024]{1,0:T(8,128)(2,1)S(1)}, bf16[256,1024]{1,0:T(8,128)(2,1)S(1)}, u32[]{:S(2)}, u32[]{:S(2)}) collective-permute-start(bf16[256,1024]{1,0:T(8,128)(2,1)S(1)} %get-tuple-element.106), channel_id=1, source_target_pairs={{0,1},{1,0},{2,3},{3,2},{4,5},{5,4},{6,7},{7,6},{8,9},{9,8},{10,11... | collective-permute-start | bytes 1572872 | tf_op jit(solution)/shard_map/ppermute | solution.py:931
  96.4 25.9 %collective-permute-start.21 = (bf16[256,1024]{1,0:T(8,128)(2,1)S(1)}, bf16[256,1024]{1,0:T(8,128)(2,1)S(1)}, u32[]{:S(2)}, u32[]{:S(2)}) collective-permute-start(bf16[256,1024]{1,0:T(8,128)(2,1)S(1)} %get-tuple-element.103), channel_id=1, source_target_pairs={{0,1},{1,0},{2,3},{3,2},{4,5},{5,4},{6,7},{7,6},{8,9},{9,8},{10,11... | collective-permute-start | bytes 1572872 | tf_op jit(solution)/shard_map/ppermute | solution.py:931
  101.8 37.9 %collective-permute-start.28 = (bf16[256,1024]{1,0:T(8,128)(2,1)S(1)}, bf16[256,1024]{1,0:T(8,128)(2,1)S(1)}, u32[]{:S(2)}, u32[]{:S(2)}) collective-permute-start(bf16[256,1024]{1,0:T(8,128)(2,1)S(1)} %add_convert_fusion.4), channel_id=1, source_target_pairs={{0,2},{1,3},{2,0},{3,1},{4,6},{5,7},{6,4},{7,5},{8,10},{9,11},{10,... | collective-permute-start | bytes 1572872 | tf_op jit(solution)/shard_map/ppermute | solution.py:931
  122.5 27.2 %collective-permute-start.25 = (bf16[256,1024]{1,0:T(8,128)(2,1)S(1)}, bf16[256,1024]{1,0:T(8,128)(2,1)S(1)}, u32[]{:S(2)}, u32[]{:S(2)}) collective-permute-start(bf16[256,1024]{1,0:T(8,128)(2,1)S(1)} %add_convert_fusion.6), channel_id=1, source_target_pairs={{0,2},{1,3},{2,0},{3,1},{4,6},{5,7},{6,4},{7,5},{8,10},{9,11},{10,... | collective-permute-start | bytes 1572872 | tf_op jit(solution)/shard_map/ppermute | solution.py:931
  126.0 38.7 %collective-permute-start.22 = (bf16[512,1024]{1,0:T(8,128)(2,1)S(1)}, bf16[512,1024]{1,0:T(8,128)(2,1)S(1)}, u32[]{:S(2)}, u32[]{:S(2)}) collective-permute-start(bf16[512,1024]{1,0:T(8,128)(2,1)S(1)} %get-tuple-element.104), channel_id=1, source_target_pairs={{0,1},{1,0},{2,3},{3,2},{4,5},{5,4},{6,7},{7,6},{8,9},{9,8},{10,11... | collective-permute-start | bytes 3145736 | tf_op jit(solution)/shard_map/ppermute | solution.py:931
  140.0 51.8 %collective-permute-start.29 = (bf16[256,1024]{1,0:T(8,128)(2,1)S(1)}, bf16[256,1024]{1,0:T(8,128)(2,1)S(1)}, u32[]{:S(2)}, u32[]{:S(2)}) collective-permute-start(bf16[256,1024]{1,0:T(8,128)(2,1)S(1)} %add_convert_fusion.3.refs_2_), channel_id=1, source_target_pairs={{0,1},{1,0},{2,3},{3,2},{4,5},{5,4},{6,7},{7,6},{8,9},{9,8},{10,11... | collective-permute-start | bytes 1572872 | tf_op jit(solution)/shard_map/ppermute | solution.py:931
  149.9 51.7 %collective-permute-start.26 = (bf16[256,1024]{1,0:T(8,128)(2,1)S(1)}, bf16[256,1024]{1,0:T(8,128)(2,1)S(1)}, u32[]{:S(2)}, u32[]{:S(2)}) collective-permute-start(bf16[256,1024]{1,0:T(8,128)(2,1)S(1)} %add_convert_fusion.5.refs_0_), channel_id=1, source_target_pairs={{0,1},{1,0},{2,3},{3,2},{4,5},{5,4},{6,7},{7,6},{8,9},{9,8},{10,11... | collective-permute-start | bytes 1572872 | tf_op jit(solution)/shard_map/ppermute | solution.py:931
  156.6 64.4 %collective-permute-start.41 = (bf16[4,128,2048]{2,1,0:T(8,128)(2,1)S(1)}, bf16[4,128,2048]{2,1,0:T(8,128)(2,1)}, u32[]{:S(2)}, u32[]{:S(2)}) collective-permute-start(bf16[4,128,2048]{2,1,0:T(8,128)(2,1)S(1)} %get-tuple-element.151), channel_id=1, source_target_pairs={{0,4},{4,0},{8,12},{12,8},{16,20},{20,16},{24,28},{28,24},{1,5},{5... | collective-permute-start | bytes 6291464 | tf_op jit(solution)/shard_map/ppermute | solution.py:890
  165.1 55.4 %collective-permute-start.23 = (bf16[512,1024]{1,0:T(8,128)(2,1)S(1)}, bf16[512,1024]{1,0:T(8,128)(2,1)S(1)}, u32[]{:S(2)}, u32[]{:S(2)}) collective-permute-start(bf16[512,1024]{1,0:T(8,128)(2,1)S(1)} %add_convert_fusion.2), channel_id=1, source_target_pairs={{0,2},{1,3},{2,0},{3,1},{4,6},{5,7},{6,4},{7,5},{8,10},{9,11},{10,... | collective-permute-start | bytes 3145736 | tf_op jit(solution)/shard_map/ppermute | solution.py:931
  223.6 51.3 %collective-permute-start.24 = (bf16[512,1024]{1,0:T(8,128)(2,1)S(1)}, bf16[512,1024]{1,0:T(8,128)(2,1)S(1)}, u32[]{:S(2)}, u32[]{:S(2)}) collective-permute-start(bf16[512,1024]{1,0:T(8,128)(2,1)S(1)} %add_convert_fusion.1.refs_2_), channel_id=1, source_target_pairs={{0,1},{1,0},{2,3},{3,2},{4,5},{5,4},{6,7},{7,6},{8,9},{9,8},{10,11... | collective-permute-start | bytes 3145736 | tf_op jit(solution)/shard_map/ppermute | solution.py:931
  224.2 17.1 %collective-permute-start.31 = (bf16[128,1024]{1,0:T(8,128)(2,1)S(1)}, bf16[128,1024]{1,0:T(8,128)(2,1)S(1)}, u32[]{:S(2)}, u32[]{:S(2)}) collective-permute-start(bf16[128,1024]{1,0:T(8,128)(2,1)S(1)} %get-tuple-element.168), channel_id=1, source_target_pairs={{0,8},{4,12},{8,0},{12,4},{16,24},{20,28},{24,16},{28,20},{1,9},{5... | collective-permute-start | bytes 786440 | tf_op jit(solution)/shard_map/ppermute | solution.py:890
  226.2 15.1 %collective-permute-start.32 = (bf16[128,1024]{1,0:T(8,128)(2,1)S(1)}, bf16[128,1024]{1,0:T(8,128)(2,1)S(1)}, u32[]{:S(2)}, u32[]{:S(2)}) collective-permute-start(bf16[128,1024]{1,0:T(8,128)(2,1)S(1)} %get-tuple-element.170), channel_id=1, source_target_pairs={{0,16},{4,20},{8,24},{12,28},{16,0},{20,4},{24,8},{28,12},{1,17},{... | collective-permute-start | bytes 786440 | tf_op jit(solution)/shard_map/ppermute | solution.py:890
  226.7 14.6 %collective-permute-start.33 = (bf16[128,1024]{1,0:T(8,128)(2,1)S(1)}, bf16[128,1024]{1,0:T(8,128)(2,1)S(1)}, u32[]{:S(2)}, u32[]{:S(2)}) collective-permute-start(bf16[128,1024]{1,0:T(8,128)(2,1)S(1)} %get-tuple-element.169), channel_id=1, source_target_pairs={{0,24},{4,28},{8,16},{12,20},{16,8},{20,12},{24,0},{28,4},{1,25},{... | collective-permute-start | bytes 786440 | tf_op jit(solution)/shard_map/ppermute | solution.py:890
  241.5 17.6 %collective-permute-start.34 = (bf16[128,1024]{1,0:T(8,128)(2,1)S(1)}, bf16[128,1024]{1,0:T(8,128)(2,1)S(1)}, u32[]{:S(2)}, u32[]{:S(2)}) collective-permute-start(bf16[128,1024]{1,0:T(8,128)(2,1)S(1)} %fusion.8.refs_0_), channel_id=1, source_target_pairs={{0,2},{1,3},{2,0},{3,1},{4,6},{5,7},{6,4},{7,5},{8,10},{9,11},{10,... | collective-permute-start | bytes 786440 | tf_op jit(solution)/shard_map/ppermute | solution.py:931
  243.5 31.4 %collective-permute-start.35 = (bf16[128,1024]{1,0:T(8,128)(2,1)S(1)}, bf16[128,1024]{1,0:T(8,128)(2,1)S(1)}, u32[]{:S(2)}, u32[]{:S(2)}) collective-permute-start(bf16[128,1024]{1,0:T(8,128)(2,1)S(1)} %fusion.8.refs_0_), channel_id=1, source_target_pairs={{0,1},{1,0},{2,3},{3,2},{4,5},{5,4},{6,7},{7,6},{8,9},{9,8},{10,11... | collective-permute-start | bytes 786440 | tf_op jit(solution)/shard_map/ppermute | solution.py:931
  243.6 32.5 %collective-permute-start.42 = (bf16[2,128,2048]{2,1,0:T(8,128)(2,1)S(1)}, bf16[2,128,2048]{2,1,0:T(8,128)(2,1)S(1)}, u32[]{:S(2)}, u32[]{:S(2)}) collective-permute-start(bf16[2,128,2048]{2,1,0:T(8,128)(2,1)S(1)} %copy-done.80), channel_id=1, source_target_pairs={{0,8},{4,12},{8,0},{12,4},{16,24},{20,28},{24,16},{28,20},{1,9},{5... | collective-permute-start | bytes 3145736 | tf_op jit(solution)/shard_map/ppermute | solution.py:890
  259.0 15.8 %collective-permute-start.36 = (bf16[128,1024]{1,0:T(8,128)(2,1)S(1)}, bf16[128,1024]{1,0:T(8,128)(2,1)S(1)}, u32[]{:S(2)}, u32[]{:S(2)}) collective-permute-start(bf16[128,1024]{1,0:T(8,128)(2,1)S(1)} %collective-permute-done.34.refs_2_), channel_id=1, source_target_pairs={{0,1},{1,0},{2,3},{3,2},{4,5},{5,4},{6,7},{7,6},{8,9},{9,8},{10,11... | collective-permute-start | bytes 786440 | tf_op jit(solution)/shard_map/ppermute | solution.py:931
  277.9 14.7 %collective-permute-start.43 = (bf16[128,2048]{1,0:T(8,128)(2,1)S(1)}, bf16[128,2048]{1,0:T(8,128)(2,1)S(1)}, u32[]{:S(2)}, u32[]{:S(2)}) collective-permute-start(bf16[128,2048]{1,0:T(8,128)(2,1)S(1)} %fusion.4), channel_id=1, source_target_pairs={{0,16},{4,20},{8,24},{12,28},{16,0},{20,4},{24,8},{28,12},{1,17},{... | collective-permute-start | bytes 1572872 | tf_op jit(solution)/shard_map/ppermute | solution.py:890
  (101 other events, 1482.9 us)
